TPU v7x, 256 devices: a whole 4x4x8 slice. The times are simulated.
256 devices in a mesh: sta: 64 (over z, y, core), win: 4 (over x).
Axes of the slice: x: 4, y: 4, z: 8, core: 2. Of those that a mesh axis runs over, the one named last changes fastest.
Arguments:
- spectra: float32 [4, 1024, 8192], P('win', 'sta')
- wanted: int32 [64, 64, 3], P('sta'), may hold values from 0 to 15, as said below
- pairs: int32 [16384, 2], P('sta'), may hold values from 0 to 191, as said below
- counts: int32 [64], P('sta'), may hold values from 32 to 256, as said below
Outputs:
- correlations: float32 [16384, 1024], P(('sta', 'win'))
Inputs may be any that keep to these rules, and one draw needn't show every extreme that they name: `wanted`: each source's 3 entries for one owner are distinct local stations. `pairs`: the two entries of a pair slot differ. `counts`: some owner has all 256 slots live in every draw.
All inputs are finite; a program needn't handle non-finite values.
Results may differ from a plain program's by a relative error of at most 0.0043.
Values may be sent and summed in bfloat16 or wider, within the bound.
A program may use at most 128 MiB of HBM per device.

v0:
```python
import math

import jax
import jax.numpy as jnp
from jax import lax
from jax.sharding import PartitionSpec as P

BAND = 64
LAGS = 1024
FREQ_BLOCK = 512


def whiten(spectra):
    width = spectra.shape[-1] // 2
    real_part = spectra[..., :width]
    imag_part = spectra[..., width:]
    magnitude = jnp.sqrt(real_part * real_part + imag_part * imag_part)
    shape = magnitude.shape[:-1] + (width // BAND, BAND)
    band = jnp.mean(magnitude.reshape(shape), axis=-1) + 1e-06
    band = jnp.repeat(band, BAND, axis=-1)
    scale = jnp.concatenate([band, band], axis=-1)
    return (spectra / scale).astype(jnp.bfloat16)


def cross_of(left, right):
    width = left.shape[-1] // 2
    left = left.astype(jnp.float32)
    right = right.astype(jnp.float32)
    lre, lim = (left[..., :width], left[..., width:])
    rre, rim = (right[..., :width], right[..., width:])
    return jnp.concatenate([lre * rre + lim * rim, lre * rim - lim * rre], axis=-1)


def inverse(stack):
    width = stack.shape[1] // 2
    real_part = stack[:, :width]
    imag_part = stack[:, width:]
    lag_index = jnp.arange(LAGS, dtype=jnp.int32) - LAGS // 2
    period = 2 * width

    def step(block, total):
        start = (block * FREQ_BLOCK).astype(jnp.int32)
        freq = start + jnp.arange(FREQ_BLOCK, dtype=jnp.int32)
        phase = jnp.mod(freq[:, None] * lag_index[None, :], period)
        angle = phase.astype(jnp.float32) * (2.0 * math.pi / period)
        re_block = lax.dynamic_slice_in_dim(real_part, start, FREQ_BLOCK, 1)
        im_block = lax.dynamic_slice_in_dim(imag_part, start, FREQ_BLOCK, 1)
        total = total + jnp.dot(
            re_block,
            jnp.cos(angle),
            precision=lax.Precision.HIGHEST,
            preferred_element_type=jnp.float32,
        )
        total = total - jnp.dot(
            im_block,
            jnp.sin(angle),
            precision=lax.Precision.HIGHEST,
            preferred_element_type=jnp.float32,
        )
        return total

    zeros = jnp.zeros((stack.shape[0], LAGS), jnp.float32)
    total = lax.fori_loop(0, width // FREQ_BLOCK, step, zeros)
    return total / math.sqrt(width)


def local(spectra, wanted, pairs, counts):
    white = whiten(spectra)
    owners = wanted.shape[1]
    per_owner = wanted.shape[2]
    windows_here = white.shape[0]
    span = white.shape[2]
    table = wanted[0].reshape(owners * per_owner)
    outgoing = jnp.take(white, table, axis=1).reshape(windows_here, owners, per_owner, span)
    received = lax.all_to_all(outgoing, "sta", split_axis=1, concat_axis=1, tiled=True)
    items = received.shape[0]
    flat = received.reshape(items, owners * per_owner, span)
    left = jnp.take(flat, pairs[:, 0], axis=1)
    right = jnp.take(flat, pairs[:, 1], axis=1)
    crosses = cross_of(left, right)
    stack = jnp.sum(crosses, axis=0)
    slot_total = pairs.shape[0]
    share = slot_total // lax.axis_size("win")
    mine = lax.psum_scatter(stack, "win", scatter_dimension=0, tiled=True)
    corr = inverse(mine)
    position = lax.axis_index("win") * share + jnp.arange(share, dtype=jnp.int32)
    live = position < counts[0]
    return jnp.where(live[:, None], corr, jnp.zeros_like(corr))


def solution(mesh):
    placed = (P("win", "sta", None), P("sta", None, None), P("sta", None), P("sta"))
    return jax.shard_map(
        local, mesh=mesh, in_specs=placed, out_specs=P(("sta", "win"), None), check_vma=False
    )
```

profile of v0, /device:TPU:1, one launch (start us, length us, event | category | flops | bytes accessed | tf_op | source)
XLA Modules:
  0.0 404.2 jit_solution(17163897055009120714)
XLA Ops:
  6.5 0.0 copy-start
  6.5 0.8 copy.9
  7.4 0.7 compare_and_fusion.2
  8.1 1.1 add_sqrt_fusion
  9.2 0.2 reshape.113
  9.4 0.2 reduce_sum.13
  9.6 0.2 broadcast_in_dim.41
  9.8 0.2 broadcast_in_dim.42
  10.0 0.0 copy-done
  10.1 0.1 reshape_squeeze.6
  10.2 2.5 gather_fusion
  12.8 4.4 %gather.10 = bf16[1,64,3,8192]{3,2,1,0:T(4,128)(2,1)} reshape(bf16[192,8192]{1,0:T(8,128)(2,1)S(1)} %gather_fusion) | data formatting | bytes 6291456 | tf_op jit(solution)/shard_map/jit(_take)/gather | solution.py:74
  17.2 0.1 copy.8
  17.3 6.1 %select_bitcast_fusion = bf16[1,64,3,8192]{3,2,0,1:T(4,128)(2,1)} fusion(bf16[1,64,3,8192]{3,2,1,0:T(4,128)(2,1)} %gather.10, pred[64,3]{1,0:T(8,128)(4,1)S(1)} %copy.8), kind=kLoop, calls=%fused_computation.37 | loop fusion | flops 1572864 | bytes 6291648 | tf_op jit(solution)/shard_map/jit(_take)/select_n | solution.py:74
  23.4 0.0 copy-start.1
  23.4 13.5 %all-to-all-start = ((bf16[1,64,3,8192]{3,2,0,1:T(4,128)(2,1)}), bf16[1,64,3,8192]{3,2,0,1:T(4,128)(2,1)}, u32[]{:S(2)}, u32[]{:S(2)}) async-start(bf16[1,64,3,8192]{3,2,0,1:T(4,128)(2,1)} %select_bitcast_fusion), calls=%async_computation | async-start | bytes 8388608 | tf_op jit(solution)/shard_map/all_to_all | solution.py:75
  36.9 0.2 reduce-scatter.2.cloned.1.call-start
  37.1 0.0 copy-done.1
  37.3 94.1 %all-to-all-done = bf16[1,64,3,8192]{3,2,0,1:T(4,128)(2,1)} async-done(((bf16[1,64,3,8192]{3,2,0,1:T(4,128)(2,1)}), bf16[1,64,3,8192]{3,2,0,1:T(4,128)(2,1)}, u32[]{:S(2)}, u32[]{:S(2)}) %all-to-all-start) | async-done | bytes 3145760 | tf_op jit(solution)/shard_map/all_to_all | solution.py:75
  131.3 6.0 %reshape.148 = bf16[192,8192]{1,0:T(8,128)(2,1)S(1)} reshape(bf16[1,64,3,8192]{3,2,0,1:T(4,128)(2,1)} %all-to-all-done) | data formatting | bytes 6291456 | tf_op jit(solution)/shard_map/jit(_take)/Arg_0.7 | solution.py:78
  137.3 5.2 %gather_fusion.1 = bf16[256,8192]{1,0:T(8,128)(2,1)} fusion(bf16[192,8192]{1,0:T(8,128)(2,1)S(1)} %reshape.148, s32[1024]{0:T(1024)S(1)} %pad_clamp_fusion.1), kind=kCustom, calls=%fused_computation.clone | custom fusion | bytes 8389632 | tf_op jit(solution)/shard_map/jit(_take)/gather | solution.py:78
  142.5 5.1 %gather_fusion.2 = bf16[256,8192]{1,0:T(8,128)(2,1)} fusion(bf16[192,8192]{1,0:T(8,128)(2,1)S(1)} %reshape.148, s32[1024]{0:T(1024)S(1)} %pad_clamp_fusion), kind=kCustom, calls=%fused_computation.1.clone | custom fusion | bytes 8389632 | tf_op jit(solution)/shard_map/jit(_take)/gather | solution.py:79
  147.6 10.3 %fusion.27 = (f32[1,256,8192]{2,1,0:T(8,128)}, f32[1,256,8192]{2,1,0:T(8,128)}) fusion(bf16[256,8192]{1,0:T(8,128)(2,1)} %gather_fusion.2, pred[256]{0:T(512)(128)(4,1)S(1)} %compare_and_fusion, bf16[256,8192]{1,0:T(8,128)(2,1)} %gather_fusion.1, pred[256]{0:T(512)(128)(4,1)S(1)} %compare_and_fusion.1), kind=kLoop, calls=%fused_computation.32 | loop fusion | flops 8388608 | bytes 25166336 | tf_op jit(solution)/shard_map/convert_element_type | solution.py:28
  158.0 6.5 %multiply_add_fusion = (f32[1,256,4096]{2,1,0:T(8,128)S(1)}, f32[1,256,4096]{2,1,0:T(8,128)S(1)}) fusion(f32[1,256,8192]{2,1,0:T(8,128)} %get-tuple-element.171, f32[1,256,8192]{2,1,0:T(8,128)} %get-tuple-element.172), kind=kLoop, calls=%fused_computation.36 | loop fusion | flops 6291456 | bytes 25165824 | tf_op jit(solution)/shard_map/add | solution.py:31
  164.5 3.8 maximum_bitcast_fusion
  168.3 0.0 reduce-scatter.2.cloned.1.call-update
  169.0 80.4 %reduce-scatter.2.cloned.1.call-done = f32[64,8192]{1,0:T(8,128)} async-done(((f32[256,8192]{1,0:T(8,128)}), f32[64,8192]{1,0:T(8,128)}) %reduce-scatter.2.cloned.1.call-update) | async-done | bytes 2097168 | tf_op jit(solution)/shard_map/reduce_scatter | solution.py:84
  249.4 1.7 fusion.31
  251.1 145.4 %while.16 = (s32[]{:T(128)}, f32[64,1024]{1,0:T(8,128)S(1)}, f32[64,4096]{1,0:T(8,128)S(1)}, f32[64,4096]{1,0:T(8,128)S(1)}, s32[]{:T(128)}, /*index=5*/s32[]{:T(128)}, s32[]{:T(128)}, s32[]{:T(128)}) while((s32[]{:T(128)}, f32[64,1024]{1,0:T(8,128)S(1)}, f32[64,4096]{1,0:T(8,128)S(1)}, f32[64,4096]{1,0:T(8,128)S(1)}, s32[]{:T(128)}, ...), condition=%wide.region_3.5_spmd.clone, body=%wide.region_2.4_spmd.clone.sunk | while | flops 820184576 | bytes 1329305 | solution.py:63
  251.3 9.1 %fusion.43 = f32[64,1024]{1,0:T(8,128)S(1)} fusion(s32[1024]{0:T(1024)S(1)} %iota_add_fusion.4, s32[512]{0:T(512)S(1)} %iota_add_fusion.5, f32[64,4096]{1,0:T(8,128)S(1)} %get-tuple-element.217, s32[]{:T(128)S(6)} %select_n.126), kind=kOutput, calls=%fused_computation.12.clone.1 | convolution fusion | flops 409993216 | bytes 399364 | tf_op jit(solution)/shard_map/while/body/eval_jaxpr/dot_general | solution.py:54
  260.4 9.0 %fusion.44 = f32[64,1024]{1,0:T(8,128)S(1)} fusion(f32[64,1024]{1,0:T(8,128)S(1)} %fusion.43, s32[1024]{0:T(1024)S(1)} %iota_add_fusion.4, s32[512]{0:T(512)S(1)} %iota_add_fusion.5, f32[64,1024]{1,0:T(8,128)S(1)} %get-tuple-element.207, f32[64,4096]{1,0:T(8,128)S(1)} %get-tuple-element.216, s32[]{:T(128)S(6)} %select_n.126, pred[]{:T(512)S(6)} %compare.4), kind=kOutput, calls=%fused_computation.17.clone.1 | convolution fusion | flops 410189824 | bytes 923653 | tf_op jit(solution)/shard_map/while/body/eval_jaxpr/dot_general | solution.py:48
  269.5 9.1 %fusion.43 = f32[64,1024]{1,0:T(8,128)S(1)} fusion(s32[1024]{0:T(1024)S(1)} %iota_add_fusion.4, s32[512]{0:T(512)S(1)} %iota_add_fusion.5, f32[64,4096]{1,0:T(8,128)S(1)} %get-tuple-element.217, s32[]{:T(128)S(6)} %select_n.126), kind=kOutput, calls=%fused_computation.12.clone.1 | convolution fusion | flops 409993216 | bytes 399364 | tf_op jit(solution)/shard_map/while/body/eval_jaxpr/dot_general | solution.py:54
  278.6 9.0 %fusion.44 = f32[64,1024]{1,0:T(8,128)S(1)} fusion(f32[64,1024]{1,0:T(8,128)S(1)} %fusion.43, s32[1024]{0:T(1024)S(1)} %iota_add_fusion.4, s32[512]{0:T(512)S(1)} %iota_add_fusion.5, f32[64,1024]{1,0:T(8,128)S(1)} %get-tuple-element.207, f32[64,4096]{1,0:T(8,128)S(1)} %get-tuple-element.216, s32[]{:T(128)S(6)} %select_n.126, pred[]{:T(512)S(6)} %compare.4), kind=kOutput, calls=%fused_computation.17.clone.1 | convolution fusion | flops 410189824 | bytes 923653 | tf_op jit(solution)/shard_map/while/body/eval_jaxpr/dot_general | solution.py:48
  287.6 9.1 %fusion.43 = f32[64,1024]{1,0:T(8,128)S(1)} fusion(s32[1024]{0:T(1024)S(1)} %iota_add_fusion.4, s32[512]{0:T(512)S(1)} %iota_add_fusion.5, f32[64,4096]{1,0:T(8,128)S(1)} %get-tuple-element.217, s32[]{:T(128)S(6)} %select_n.126), kind=kOutput, calls=%fused_computation.12.clone.1 | convolution fusion | flops 409993216 | bytes 399364 | tf_op jit(solution)/shard_map/while/body/eval_jaxpr/dot_general | solution.py:54
  296.7 9.0 %fusion.44 = f32[64,1024]{1,0:T(8,128)S(1)} fusion(f32[64,1024]{1,0:T(8,128)S(1)} %fusion.43, s32[1024]{0:T(1024)S(1)} %iota_add_fusion.4, s32[512]{0:T(512)S(1)} %iota_add_fusion.5, f32[64,1024]{1,0:T(8,128)S(1)} %get-tuple-element.207, f32[64,4096]{1,0:T(8,128)S(1)} %get-tuple-element.216, s32[]{:T(128)S(6)} %select_n.126, pred[]{:T(512)S(6)} %compare.4), kind=kOutput, calls=%fused_computation.17.clone.1 | convolution fusion | flops 410189824 | bytes 923653 | tf_op jit(solution)/shard_map/while/body/eval_jaxpr/dot_general | solution.py:48
  305.8 9.1 %fusion.43 = f32[64,1024]{1,0:T(8,128)S(1)} fusion(s32[1024]{0:T(1024)S(1)} %iota_add_fusion.4, s32[512]{0:T(512)S(1)} %iota_add_fusion.5, f32[64,4096]{1,0:T(8,128)S(1)} %get-tuple-element.217, s32[]{:T(128)S(6)} %select_n.126), kind=kOutput, calls=%fused_computation.12.clone.1 | convolution fusion | flops 409993216 | bytes 399364 | tf_op jit(solution)/shard_map/while/body/eval_jaxpr/dot_general | solution.py:54
  314.9 9.0 %fusion.44 = f32[64,1024]{1,0:T(8,128)S(1)} fusion(f32[64,1024]{1,0:T(8,128)S(1)} %fusion.43, s32[1024]{0:T(1024)S(1)} %iota_add_fusion.4, s32[512]{0:T(512)S(1)} %iota_add_fusion.5, f32[64,1024]{1,0:T(8,128)S(1)} %get-tuple-element.207, f32[64,4096]{1,0:T(8,128)S(1)} %get-tuple-element.216, s32[]{:T(128)S(6)} %select_n.126, pred[]{:T(512)S(6)} %compare.4), kind=kOutput, calls=%fused_computation.17.clone.1 | convolution fusion | flops 410189824 | bytes 923653 | tf_op jit(solution)/shard_map/while/body/eval_jaxpr/dot_general | solution.py:48
  323.9 9.1 %fusion.43 = f32[64,1024]{1,0:T(8,128)S(1)} fusion(s32[1024]{0:T(1024)S(1)} %iota_add_fusion.4, s32[512]{0:T(512)S(1)} %iota_add_fusion.5, f32[64,4096]{1,0:T(8,128)S(1)} %get-tuple-element.217, s32[]{:T(128)S(6)} %select_n.126), kind=kOutput, calls=%fused_computation.12.clone.1 | convolution fusion | flops 409993216 | bytes 399364 | tf_op jit(solution)/shard_map/while/body/eval_jaxpr/dot_general | solution.py:54
  333.0 9.0 %fusion.44 = f32[64,1024]{1,0:T(8,128)S(1)} fusion(f32[64,1024]{1,0:T(8,128)S(1)} %fusion.43, s32[1024]{0:T(1024)S(1)} %iota_add_fusion.4, s32[512]{0:T(512)S(1)} %iota_add_fusion.5, f32[64,1024]{1,0:T(8,128)S(1)} %get-tuple-element.207, f32[64,4096]{1,0:T(8,128)S(1)} %get-tuple-element.216, s32[]{:T(128)S(6)} %select_n.126, pred[]{:T(512)S(6)} %compare.4), kind=kOutput, calls=%fused_computation.17.clone.1 | convolution fusion | flops 410189824 | bytes 923653 | tf_op jit(solution)/shard_map/while/body/eval_jaxpr/dot_general | solution.py:48
  342.1 9.1 %fusion.43 = f32[64,1024]{1,0:T(8,128)S(1)} fusion(s32[1024]{0:T(1024)S(1)} %iota_add_fusion.4, s32[512]{0:T(512)S(1)} %iota_add_fusion.5, f32[64,4096]{1,0:T(8,128)S(1)} %get-tuple-element.217, s32[]{:T(128)S(6)} %select_n.126), kind=kOutput, calls=%fused_computation.12.clone.1 | convolution fusion | flops 409993216 | bytes 399364 | tf_op jit(solution)/shard_map/while/body/eval_jaxpr/dot_general | solution.py:54
  351.2 9.0 %fusion.44 = f32[64,1024]{1,0:T(8,128)S(1)} fusion(f32[64,1024]{1,0:T(8,128)S(1)} %fusion.43, s32[1024]{0:T(1024)S(1)} %iota_add_fusion.4, s32[512]{0:T(512)S(1)} %iota_add_fusion.5, f32[64,1024]{1,0:T(8,128)S(1)} %get-tuple-element.207, f32[64,4096]{1,0:T(8,128)S(1)} %get-tuple-element.216, s32[]{:T(128)S(6)} %select_n.126, pred[]{:T(512)S(6)} %compare.4), kind=kOutput, calls=%fused_computation.17.clone.1 | convolution fusion | flops 410189824 | bytes 923653 | tf_op jit(solution)/shard_map/while/body/eval_jaxpr/dot_general | solution.py:48
  360.3 9.1 %fusion.43 = f32[64,1024]{1,0:T(8,128)S(1)} fusion(s32[1024]{0:T(1024)S(1)} %iota_add_fusion.4, s32[512]{0:T(512)S(1)} %iota_add_fusion.5, f32[64,4096]{1,0:T(8,128)S(1)} %get-tuple-element.217, s32[]{:T(128)S(6)} %select_n.126), kind=kOutput, calls=%fused_computation.12.clone.1 | convolution fusion | flops 409993216 | bytes 399364 | tf_op jit(solution)/shard_map/while/body/eval_jaxpr/dot_general | solution.py:54
  369.3 9.0 %fusion.44 = f32[64,1024]{1,0:T(8,128)S(1)} fusion(f32[64,1024]{1,0:T(8,128)S(1)} %fusion.43, s32[1024]{0:T(1024)S(1)} %iota_add_fusion.4, s32[512]{0:T(512)S(1)} %iota_add_fusion.5, f32[64,1024]{1,0:T(8,128)S(1)} %get-tuple-element.207, f32[64,4096]{1,0:T(8,128)S(1)} %get-tuple-element.216, s32[]{:T(128)S(6)} %select_n.126, pred[]{:T(512)S(6)} %compare.4), kind=kOutput, calls=%fused_computation.17.clone.1 | convolution fusion | flops 410189824 | bytes 923653 | tf_op jit(solution)/shard_map/while/body/eval_jaxpr/dot_general | solution.py:48
  378.4 9.1 %fusion.43 = f32[64,1024]{1,0:T(8,128)S(1)} fusion(s32[1024]{0:T(1024)S(1)} %iota_add_fusion.4, s32[512]{0:T(512)S(1)} %iota_add_fusion.5, f32[64,4096]{1,0:T(8,128)S(1)} %get-tuple-element.217, s32[]{:T(128)S(6)} %select_n.126), kind=kOutput, calls=%fused_computation.12.clone.1 | convolution fusion | flops 409993216 | bytes 399364 | tf_op jit(solution)/shard_map/while/body/eval_jaxpr/dot_general | solution.py:54
  387.5 9.0 %fusion.44 = f32[64,1024]{1,0:T(8,128)S(1)} fusion(f32[64,1024]{1,0:T(8,128)S(1)} %fusion.43, s32[1024]{0:T(1024)S(1)} %iota_add_fusion.4, s32[512]{0:T(512)S(1)} %iota_add_fusion.5, f32[64,1024]{1,0:T(8,128)S(1)} %get-tuple-element.207, f32[64,4096]{1,0:T(8,128)S(1)} %get-tuple-element.216, s32[]{:T(128)S(6)} %select_n.126, pred[]{:T(512)S(6)} %compare.4), kind=kOutput, calls=%fused_computation.17.clone.1 | convolution fusion | flops 410189824 | bytes 923653 | tf_op jit(solution)/shard_map/while/body/eval_jaxpr/dot_general | solution.py:48
  396.5 0.8 multiply_select_fusion.1
  (29 shorter events, 0.2 us)
Async XLA Ops:
  6.5 3.5 copy-start
  23.4 13.7 %copy-start.1 = (s32[256,2]{0,1:T(2,128)S(1)}, s32[256,2]{0,1:T(2,128)}, u32[]{:S(2)}) copy-start(s32[256,2]{0,1:T(2,128)} %param.10) | copy-start | bytes 6148
  23.4 107.9 %all-to-all-start = ((bf16[1,64,3,8192]{3,2,0,1:T(4,128)(2,1)}), bf16[1,64,3,8192]{3,2,0,1:T(4,128)(2,1)}, u32[]{:S(2)}, u32[]{:S(2)}) async-start(bf16[1,64,3,8192]{3,2,0,1:T(4,128)(2,1)} %select_bitcast_fusion), calls=%async_computation | async-start | bytes 8388608 | tf_op jit(solution)/shard_map/all_to_all | solution.py:75
  36.9 212.5 %reduce-scatter.2.cloned.1.call-start = ((), (), s32[]{:S(2)}) async-start(), calls=%async_computation.2 | async-start | bytes 10485760 | tf_op jit(solution)/shard_map/reduce_scatter | solution.py:84
Sparse Core Ops, SparseCore 0:
  168.5 80.8 reduce-scatter.1
where the time goes:
time: 405 us; the launch traced here: 404 us
  waiting for transfers between devices  174 us (43%)
  matrix products  145 us (36%)
  other arithmetic  29.8 us (7%)
  local copies, waits for them, and re-layouts  26.6 us (7%)
  between operations  14.2 us (4%)
  starting transfers between devices  13.7 us (3%)
    all_to_all x1, waiting for transfers between devices, local(): lax.all_to_all(outgoing, 'sta', split_axis=1, concat_axis=1, tiled=True)  94.1 us
    reduce_scatter x1, waiting for transfers between devices, local(): mine = lax.psum_scatter(stack, 'win', scatter_dimension=0, tiled=True)  80.4 us
    dot_general x8, matrix products, step(): jnp.dot(im_block, jnp.sin(angle), precision=lax.Precision.HIGHEST, prefer...  72.7 us
    dot_general x8, matrix products, step(): jnp.dot(re_block, jnp.cos(angle), precision=lax.Precision.HIGHEST, prefer...  72.2 us
    all_to_all x1, starting transfers between devices, local(): lax.all_to_all(outgoing, 'sta', split_axis=1, concat_axis=1, tiled=True)  13.5 us
    convert_element_type x1, other arithmetic, cross_of(): right = right.astype(jnp.float32)  10.3 us
  transfers between devices with their start and end apart: 2, of which 2 were waited for; matrix products, arithmetic and copies ran while one was open for 0% of the time, Pallas kernels for 0%

commit v1 on v0

v1 whole, which is shorter than its diff:
```python
import math

import jax
import jax.numpy as jnp
import numpy as np
from jax import lax
from jax.sharding import PartitionSpec as P

BAND = 64
LAGS = 1024


def whiten(spectra):
    width = spectra.shape[-1] // 2
    real_part = spectra[..., :width]
    imag_part = spectra[..., width:]
    magnitude = jnp.sqrt(real_part * real_part + imag_part * imag_part)
    shape = magnitude.shape[:-1] + (width // BAND, BAND)
    band = jnp.mean(magnitude.reshape(shape), axis=-1) + 1e-06
    band = jnp.repeat(band, BAND, axis=-1)
    scale = jnp.concatenate([band, band], axis=-1)
    return (spectra / scale).astype(jnp.bfloat16)


def tables(width, parts):
    quarter = width // parts
    fine = 32
    lag = np.arange(LAGS, dtype=np.int64) - LAGS // 2
    period = 2 * width

    def both(freq):
        angle = (freq[:, None] * lag[None, :]) % period * (2.0 * np.pi / period)
        return np.stack([np.cos(angle), np.sin(angle)]).astype(np.float32)

    return both(np.arange(fine)), both(np.arange(0, width, fine)).reshape(2, parts, quarter // fine, LAGS)


def local(spectra, wanted, pairs, counts):
    white = whiten(spectra)[0]
    owners = wanted.shape[1]
    per_owner = wanted.shape[2]
    width = white.shape[1] // 2
    parts = lax.axis_size("win")
    me = lax.axis_index("win")
    quarter = width // parts
    stations = white.shape[0]
    split = white.reshape(stations, 2, parts, quarter)
    split = jnp.transpose(split, (2, 0, 1, 3))
    split = lax.all_to_all(split, "win", split_axis=0, concat_axis=0, tiled=True)
    mixed = jnp.transpose(split, (1, 0, 2, 3)).reshape(stations, parts * 2 * quarter)
    outgoing = jnp.take(mixed, wanted[0].reshape(-1), axis=0)
    received = lax.all_to_all(outgoing, "sta", split_axis=0, concat_axis=0, tiled=True)
    left = jnp.take(received, pairs[:, 0], axis=0).reshape(-1, parts, 2, quarter).astype(jnp.float32)
    right = jnp.take(received, pairs[:, 1], axis=0).reshape(-1, parts, 2, quarter).astype(jnp.float32)
    lre, lim = left[:, :, 0], left[:, :, 1]
    rre, rim = right[:, :, 0], right[:, :, 1]
    stack_re = jnp.sum(lre * rre + lim * rim, axis=1)
    stack_im = jnp.sum(lre * rim - lim * rre, axis=1)
    fine, coarse = tables(width, parts)
    mine = lax.dynamic_index_in_dim(jnp.asarray(coarse), me, 1, keepdims=False)
    cc, sc = mine[0][:, None], mine[1][:, None]
    cf, sf = fine[0][None], fine[1][None]
    cos = (cc * cf - sc * sf).reshape(quarter, LAGS)
    sin = (sc * cf + cc * sf).reshape(quarter, LAGS)
    stack = jnp.concatenate([stack_re, stack_im], axis=1)
    wave = jnp.concatenate([cos, -sin], axis=0)
    partial = jnp.dot(stack, wave, precision=lax.Precision.HIGHEST, preferred_element_type=jnp.float32)
    corr = lax.psum_scatter(partial, "win", scatter_dimension=0, tiled=True) / math.sqrt(width)
    share = corr.shape[0]
    position = me * share + jnp.arange(share, dtype=jnp.int32)
    live = position < counts[0]
    return jnp.where(live[:, None], corr, jnp.zeros_like(corr))


def solution(mesh):
    placed = (P("win", "sta", None), P("sta", None, None), P("sta", None), P("sta"))
    return jax.shard_map(
        local, mesh=mesh, in_specs=placed, out_specs=P(("sta", "win"), None), check_vma=False
    )
```

time: 405 us -> 269 us (0.66)
  matrix products: 145 us -> 8.28 us
  waiting for transfers between devices: 174 us -> 114 us
  other arithmetic: 29.8 us -> 61.4 us
  local copies, waits for them, and re-layouts: 26.6 us -> 50.2 us
  starting transfers between devices: 13.7 us -> 19 us
    dot_general x16 -> x1, matrix products: 145 us -> 8.28 us  [local(): jnp.dot(stack, wave, precision=lax.Precision.HIGHEST, preferred_element_t...]
    reduce_scatter x1, waiting for transfers between devices: 80.4 us -> 20.1 us  [local(): lax.psum_scatter(partial, 'win', scatter_dimension=0, tiled=True)]
    reduce_sum x1, other arithmetic: 3.8 us -> 34.6 us  [local(): stack_re = jnp.sum(lre * rre + lim * rim, axis=1)]
    convert_element_type x0 -> x2, local copies, waits for them, and re-layouts: none -> 23.5 us  [the longest x1 11.8 us: local(): jnp.take(received, pairs[:, 0], axis=0).reshape(-1, parts, 2, quarter)]
    add x9 -> x0, other arithmetic: 6.57 us -> none  [the longest x1 6.54 us: cross_of(): lre * rre + lim * rim]
    all_to_all x0 -> x1, local copies, waits for them, and re-layouts: none -> 5.99 us  [local(): lax.all_to_all(outgoing, 'sta', split_axis=0, concat_axis=0, tiled=True)]
    another operation x2, local copies, waits for them, and re-layouts: 6.12 us -> 0.31 us  [the longest x1 0.18 us: local(): split = white.reshape(stations, 2, parts, quarter)]
    all_to_all x1 -> x2, starting transfers between devices: 13.5 us -> 18.9 us  [the longest x1 14.1 us: local(): lax.all_to_all(outgoing, 'sta', split_axis=0, concat_axis=0, tiled=True)]
  transfers between devices with their start and end apart: 2 -> 3, of which waited for: 2 -> 3; matrix products, arithmetic and copies ran while one was open for 0% -> 2% of each run, Pallas kernels for 0% -> 0%
where the time goes in v1:
time: 269 us; the launch traced here: 267 us
  waiting for transfers between devices  114 us (42%)
  other arithmetic  61.4 us (23%)
  local copies, waits for them, and re-layouts  50.2 us (19%)
  starting transfers between devices  19 us (7%)
  between operations  14.3 us (5%)
  matrix products  8.28 us (3%)
    all_to_all x1, waiting for transfers between devices, local(): lax.all_to_all(outgoing, 'sta', split_axis=0, concat_axis=0, tiled=True)  88.8 us
    reduce_sum x1, other arithmetic, local(): stack_re = jnp.sum(lre * rre + lim * rim, axis=1)  34.6 us
    reduce_scatter x1, waiting for transfers between devices, local(): lax.psum_scatter(partial, 'win', scatter_dimension=0, tiled=True)  20.1 us
    all_to_all x1, starting transfers between devices, local(): lax.all_to_all(outgoing, 'sta', split_axis=0, concat_axis=0, tiled=True)  14.1 us
    convert_element_type x1, local copies, waits for them, and re-layouts, local(): jnp.take(received, pairs[:, 0], axis=0).reshape(-1, parts, 2, quarter)  11.8 us
    convert_element_type x1, local copies, waits for them, and re-layouts, local(): jnp.take(received, pairs[:, 1], axis=0).reshape(-1, parts, 2, quarter)  11.8 us
    dot_general x1, matrix products, local(): jnp.dot(stack, wave, precision=lax.Precision.HIGHEST, preferred_element_t...  8.28 us
    gather x2, local copies, waits for them, and re-layouts, local(): outgoing = jnp.take(mixed, wanted[0].reshape(-1), axis=0)  6.96 us
  transfers between devices with their start and end apart: 3, of which 3 were waited for; matrix products, arithmetic and copies ran while one was open for 2% of the time, Pallas kernels for 0%

profile of v1, /device:TPU:1, one launch (start us, length us, event | category | flops | bytes accessed | tf_op | source)
XLA Modules:
  0.0 267.1 jit_solution(15624824532072688701)
XLA Ops:
  6.5 0.0 copy-start.4
  6.5 1.1 add_sqrt_fusion
  7.7 0.2 reshape.104
  7.9 0.2 reduce_sum.27
  8.1 0.2 broadcast_in_dim.38
  8.3 0.2 broadcast_in_dim.39
  8.5 1.1 fusion.7
  9.6 0.2 reshape_squeeze.9
  9.8 0.9 copy.17
  10.7 4.8 %all-to-all-start = ((bf16[4,16,2,1024]{3,2,1,0:T(2,128)(2,1)}), bf16[4,16,2,1024]{3,2,1,0:T(2,128)(2,1)S(1)}, u32[]{:S(2)}, u32[]{:S(2)}) async-start(bf16[4,16,2,1024]{3,2,1,0:T(2,128)(2,1)} %copy.17), calls=%async_computation | async-start | bytes 524288 | tf_op jit(solution)/shard_map/all_to_all | solution.py:49
  15.5 0.0 copy-done.4
  15.5 0.1 copy.19
  15.6 0.1 reshape_squeeze.10
  15.8 0.1 copy.16
  15.9 5.1 %all-to-all-done = bf16[4,16,2,1024]{3,2,1,0:T(2,128)(2,1)S(1)} async-done(((bf16[4,16,2,1024]{3,2,1,0:T(2,128)(2,1)}), bf16[4,16,2,1024]{3,2,1,0:T(2,128)(2,1)S(1)}, u32[]{:S(2)}, u32[]{:S(2)}) %all-to-all-start) | async-done | bytes 262176 | tf_op jit(solution)/shard_map/all_to_all | solution.py:49
  21.1 0.2 copy.18
  21.3 0.2 reshape.105
  21.5 2.5 gather_fusion
  24.0 4.4 %gather.10 = bf16[64,3,8192]{2,1,0:T(4,128)(2,1)} reshape(bf16[192,8192]{1,0:T(8,128)(2,1)S(1)} %gather_fusion) | data formatting | bytes 6291456 | tf_op jit(solution)/shard_map/jit(_take)/gather | solution.py:51
  28.5 6.1 %broadcast_select_fusion = bf16[64,3,8192]{2,1,0:T(4,128)(2,1)} fusion(bf16[64,3,8192]{2,1,0:T(4,128)(2,1)} %gather.10, pred[64,3]{1,0:T(8,128)(4,1)S(1)} %copy.16), kind=kLoop, calls=%fused_computation.13 | loop fusion | flops 1572864 | bytes 6291648 | tf_op jit(solution)/shard_map/jit(_take)/select_n | solution.py:51
  34.6 0.0 copy-start.5
  34.6 0.0 copy-start.2
  34.6 0.0 copy-start.3
  34.6 14.1 %all-to-all-start.1 = ((bf16[64,3,8192]{2,1,0:T(4,128)(2,1)}), bf16[64,3,8192]{2,1,0:T(4,128)(2,1)}, u32[]{:S(2)}, u32[]{:S(2)}) async-start(bf16[64,3,8192]{2,1,0:T(4,128)(2,1)} %broadcast_select_fusion), calls=%async_computation.1 | async-start | bytes 8388608 | tf_op jit(solution)/shard_map/all_to_all | solution.py:52
  48.7 0.0 reduce-scatter.2.cloned.1.call-start
  48.7 0.0 copy-done.5
  48.8 1.0 dynamic-slice_bitcast_fusion.1
  49.8 0.0 copy-done.2
  49.8 0.0 copy-done.3
  49.9 4.4 %multiply_subtract_fusion = (f32[32,32,1024]{2,1,0:T(8,128)}, f32[32,32,1024]{2,1,0:T(8,128)}) fusion(f32[32,1024]{1,0:T(8,128)S(1)} %copy-done.2, f32[32,1024]{1,0:T(8,128)S(1)} %get-tuple-element.9, f32[32,1024]{1,0:T(8,128)S(1)} %copy-done.3, f32[32,1024]{1,0:T(8,128)S(1)} %get-tuple-element.8), kind=kLoop, calls=%fused_computation.10 | loop fusion | flops 7340032 | bytes 8912896 | tf_op jit(solution)/shard_map/sub | solution.py:63
  54.3 88.8 %all-to-all-done.1 = bf16[64,3,8192]{2,1,0:T(4,128)(2,1)} async-done(((bf16[64,3,8192]{2,1,0:T(4,128)(2,1)}), bf16[64,3,8192]{2,1,0:T(4,128)(2,1)}, u32[]{:S(2)}, u32[]{:S(2)}) %all-to-all-start.1) | async-done | bytes 3145760 | tf_op jit(solution)/shard_map/all_to_all | solution.py:52
  143.1 6.0 %all_to_all.11 = bf16[192,8192]{1,0:T(8,128)(2,1)S(1)} reshape(bf16[64,3,8192]{2,1,0:T(4,128)(2,1)} %all-to-all-done.1) | data formatting | bytes 6291456 | tf_op jit(solution)/shard_map/all_to_all | solution.py:52
  149.1 5.1 %gather_fusion.2 = bf16[256,8192]{1,0:T(8,128)(2,1)} fusion(bf16[192,8192]{1,0:T(8,128)(2,1)S(1)} %all_to_all.11, s32[1024]{0:T(1024)S(1)} %pad_clamp_fusion), kind=kCustom, calls=%fused_computation.1.clone | custom fusion | bytes 8389632 | tf_op jit(solution)/shard_map/jit(_take)/gather | solution.py:54
  154.2 5.2 %gather_fusion.1 = bf16[256,8192]{1,0:T(8,128)(2,1)} fusion(bf16[192,8192]{1,0:T(8,128)(2,1)S(1)} %all_to_all.11, s32[1024]{0:T(1024)S(1)} %pad_clamp_fusion.1), kind=kCustom, calls=%fused_computation.clone | custom fusion | bytes 8389632 | tf_op jit(solution)/shard_map/jit(_take)/gather | solution.py:53
  159.4 6.0 %select_convert_fusion.1 = f32[256,8192]{1,0:T(8,128)} fusion(bf16[256,8192]{1,0:T(8,128)(2,1)} %gather_fusion.1, pred[256]{0:T(512)(128)(4,1)S(1)} %compare_and_fusion.1), kind=kLoop, calls=%fused_computation.8 | loop fusion | flops 4194304 | bytes 12583168 | tf_op jit(solution)/shard_map/convert_element_type | solution.py:53
  165.4 11.8 %reshape.106 = f32[256,4,2,1024]{3,2,1,0:T(2,128)} reshape(f32[256,8192]{1,0:T(8,128)} %select_convert_fusion.1) | data formatting | bytes 16777216 | tf_op jit(solution)/shard_map/convert_element_type | solution.py:53
  177.1 6.0 %select_convert_fusion = f32[256,8192]{1,0:T(8,128)} fusion(bf16[256,8192]{1,0:T(8,128)(2,1)} %gather_fusion.2, pred[256]{0:T(512)(128)(4,1)S(1)} %compare_and_fusion), kind=kLoop, calls=%fused_computation.7 | loop fusion | flops 4194304 | bytes 12583168 | tf_op jit(solution)/shard_map/convert_element_type | solution.py:54
  183.2 11.8 %reshape.107 = f32[256,4,2,1024]{3,2,1,0:T(2,128)} reshape(f32[256,8192]{1,0:T(8,128)} %select_convert_fusion) | data formatting | bytes 16777216 | tf_op jit(solution)/shard_map/convert_element_type | solution.py:54
  194.9 0.0 copy-start
  194.9 0.0 copy-start.1
  194.9 34.6 %add_reduce_fusion = (f32[256,1024]{1,0:T(8,128)S(1)}, f32[256,1024]{1,0:T(8,128)S(1)}) fusion(f32[256,4,2,1024]{3,2,1,0:T(2,128)} %reshape.107, f32[256,4,2,1024]{3,2,1,0:T(2,128)} %reshape.106), kind=kLoop, calls=%fused_computation.12 | loop fusion | flops 7864320 | bytes 18874368 | tf_op jit(solution)/shard_map/reduce_sum | solution.py:57
  229.5 0.0 copy-done
  229.5 0.0 copy-done.1
  229.5 8.3 %fusion = f32[256,1024]{1,0:T(8,128)} fusion(f32[1024,1024]{1,0:T(8,128)S(1)} %bitcast.18, f32[1024,1024]{1,0:T(8,128)S(1)} %bitcast.17, f32[256,1024]{1,0:T(8,128)S(1)} %get-tuple-element.7, f32[256,1024]{1,0:T(8,128)S(1)} %get-tuple-element.6), kind=kOutput, calls=%fused_computation.3 | convolution fusion | flops 6445072384 | bytes 11534336 | tf_op jit(solution)/shard_map/dot_general | solution.py:67
  237.8 0.0 reduce-scatter.2.cloned.1.call-update
  238.5 20.1 %reduce-scatter.2.cloned.1.call-done = f32[64,1024]{1,0:T(8,128)} async-done(((f32[256,1024]{1,0:T(8,128)}), f32[64,1024]{1,0:T(8,128)}) %reduce-scatter.2.cloned.1.call-update) | async-done | bytes 262160 | tf_op jit(solution)/shard_map/reduce_scatter | solution.py:68
  258.6 1.7 multiply_select_fusion
  (12 shorter events, 0.1 us)
Async XLA Ops:
  6.5 9.0 %copy-start.4 = (s32[1,64,3]{1,0,2:T(1,128)S(1)}, s32[1,64,3]{1,0,2:T(1,128)}, u32[]{:S(2)}) copy-start(s32[1,64,3]{1,0,2:T(1,128)} %param.10) | copy-start | bytes 2308
  10.7 10.4 %all-to-all-start = ((bf16[4,16,2,1024]{3,2,1,0:T(2,128)(2,1)}), bf16[4,16,2,1024]{3,2,1,0:T(2,128)(2,1)S(1)}, u32[]{:S(2)}, u32[]{:S(2)}) async-start(bf16[4,16,2,1024]{3,2,1,0:T(2,128)(2,1)} %copy.17), calls=%async_computation | async-start | bytes 524288 | tf_op jit(solution)/shard_map/all_to_all | solution.py:49
  34.6 14.1 %copy-start.5 = (s32[256,2]{0,1:T(2,128)S(1)}, s32[256,2]{0,1:T(2,128)}, u32[]{:S(2)}) copy-start(s32[256,2]{0,1:T(2,128)} %param.11) | copy-start | bytes 6148
  34.6 15.2 %copy-start.2 = (f32[32,1024]{1,0:T(8,128)S(1)}, f32[32,1024]{1,0:T(8,128)}, u32[]{:S(2)}) copy-start(f32[32,1024]{1,0:T(8,128)} %constant.60) | copy-start | bytes 393220
  34.6 15.3 %copy-start.3 = (f32[32,1024]{1,0:T(8,128)S(1)}, f32[32,1024]{1,0:T(8,128)}, u32[]{:S(2)}) copy-start(f32[32,1024]{1,0:T(8,128)} %constant.59) | copy-start | bytes 393220
  34.6 108.5 %all-to-all-start.1 = ((bf16[64,3,8192]{2,1,0:T(4,128)(2,1)}), bf16[64,3,8192]{2,1,0:T(4,128)(2,1)}, u32[]{:S(2)}, u32[]{:S(2)}) async-start(bf16[64,3,8192]{2,1,0:T(4,128)(2,1)} %broadcast_select_fusion), calls=%async_computation.1 | async-start | bytes 8388608 | tf_op jit(solution)/shard_map/all_to_all | solution.py:52
  48.7 209.9 %reduce-scatter.2.cloned.1.call-start = ((), (), s32[]{:S(2)}) async-start(), calls=%async_computation.3 | async-start | bytes 1310720 | tf_op jit(solution)/shard_map/reduce_scatter | solution.py:68
  194.9 34.6 %copy-start = (f32[32,32,1024]{2,1,0:T(8,128)S(1)}, f32[32,32,1024]{2,1,0:T(8,128)}, u32[]{:S(2)}) copy-start(f32[32,32,1024]{2,1,0:T(8,128)} %get-tuple-element.10) | copy-start | bytes 12582916
  194.9 34.6 %copy-start.1 = (f32[32,32,1024]{2,1,0:T(8,128)S(1)}, f32[32,32,1024]{2,1,0:T(8,128)}, u32[]{:S(2)}) copy-start(f32[32,32,1024]{2,1,0:T(8,128)} %get-tuple-element.11) | copy-start | bytes 12582916
Sparse Core Ops, SparseCore 0:
  238.0 20.5 reduce-scatter.1

commit v2 on v1

v2 whole, which is shorter than its diff:
```python
import functools
import math

import jax
import jax.numpy as jnp
import numpy as np
from jax import lax
from jax.experimental import pallas as pl
from jax.experimental.pallas import tpu as pltpu
from jax.sharding import PartitionSpec as P

BAND = 64
LAGS = 1024
FINE = 32
NZ, NY, NC, NX = 8, 4, 2, 4
YC = NY * NC
STATIONS = 16
CAP = 3
WIDTH = 4096
QUARTER = WIDTH // NX
ROWS = QUARTER // 128
SLOTS = 256
SHARE = SLOTS // NX
RECV = NZ * YC * CAP
LAG_STEP = 256
SHIFT = (0, 1, 3, 2)
MESH = pl.DeviceIdType.MESH


def tables():
    lag = np.arange(LAGS, dtype=np.int64) - LAGS // 2
    period = 2 * WIDTH

    def both(freq):
        angle = (freq[:, None] * lag[None, :]) % period * (2.0 * np.pi / period)
        return np.stack([np.cos(angle), np.sin(angle)]).astype(np.float32)

    return both(np.arange(FINE)), both(np.arange(0, WIDTH, FINE))


def kernel(
    spectra, table, pairs, counts, fine_hbm, coarse_hbm, out,
    white32, quarters, held, work, stage, landed, wide, stack, lhs, wave, total, parts_out, parts_in,
    table_all, table_smem, fine, coarse,
    x_send, x_recv, z_send, z_recv, t_send, t_recv, y_send, y_recv, r_send, r_recv, local_sem, smem_sem,
):
    win = lax.axis_index("win")
    sta = lax.axis_index("sta")
    z = sta // YC
    yc = lax.rem(sta, YC)

    def at_x(step):
        return (sta, lax.rem(win + step, NX))

    def at_z(step):
        return (lax.rem(z + step + NZ, NZ) * YC + yc, win)

    def at_yc(step):
        return (z * YC + lax.rem(yc + step, YC), win)

    barrier = pltpu.get_barrier_semaphore()
    for step in (1, 2, 3):
        pl.semaphore_signal(barrier, inc=1, device_id=at_x(step), device_id_type=MESH)
    for step in (1, -1):
        pl.semaphore_signal(barrier, inc=1, device_id=at_z(step), device_id_type=MESH)
    for step in range(1, YC):
        pl.semaphore_signal(barrier, inc=1, device_id=at_yc(step), device_id_type=MESH)

    load_fine = pltpu.make_async_copy(fine_hbm, fine, local_sem.at[0])
    load_fine.start()
    own_coarse = coarse_hbm.at[:, pl.ds(pl.multiple_of(win * FINE, FINE), FINE)]
    load_coarse = pltpu.make_async_copy(own_coarse, coarse, local_sem.at[1])
    load_coarse.start()
    table_all[z] = table[...]

    lane_r = lax.broadcasted_iota(jnp.int32, (128, 128), 0) // BAND
    lane_c = lax.broadcasted_iota(jnp.int32, (128, 128), 1) // BAND
    same = jnp.where(lane_r == lane_c, 1.0, 0.0).astype(jnp.float32)
    chunks = WIDTH // 128

    @pl.loop(0, chunks // 4)
    def _(group):
        for part in range(4):
            j = group * 4 + part
            re = spectra[:, pl.ds(pl.multiple_of(j * 128, 128), 128)]
            im = spectra[:, pl.ds(pl.multiple_of(WIDTH + j * 128, 128), 128)]
            mag = jnp.sqrt(re * re + im * im)
            sums = jnp.dot(mag, same, precision=lax.Precision.HIGHEST, preferred_element_type=jnp.float32)
            band = sums * (1.0 / BAND) + 1e-06
            white32[pl.ds(j, STATIONS, stride=2 * chunks), :] = re / band
            white32[pl.ds(chunks + j, STATIONS, stride=2 * chunks), :] = im / band

    @pl.loop(0, STATIONS)
    def _(s):
        for step in range(NX):
            quarter = lax.rem(win + step, NX)
            base = s * 2 * chunks + quarter * ROWS
            re = white32[pl.ds(pl.multiple_of(base, ROWS), ROWS), :]
            im = white32[pl.ds(pl.multiple_of(base + chunks, ROWS), ROWS), :]
            slab = jnp.concatenate([re, im], axis=0).astype(jnp.bfloat16)
            if step == 0:
                held[0, z, s] = slab
            else:
                quarters[step - 1, s] = slab

    pl.semaphore_wait(barrier, 3 + 2 + YC - 1)

    def x_copy(step):
        place = SHIFT.index((NX - step) % NX)
        return pltpu.make_async_remote_copy(
            src_ref=quarters.at[step - 1], dst_ref=held.at[place, z],
            send_sem=x_send.at[place - 1], recv_sem=x_recv.at[place - 1],
            device_id=at_x(step), device_id_type=MESH,
        )

    def z_copy(i, way, k):
        source = lax.rem(z - way * k + NZ, NZ)
        ref = held.at[i, source]
        if k == NZ // 2 - 1:
            ref = ref.at[pl.ds(0 if way == 1 else STATIONS // 2, STATIONS // 2)]
        side = 0 if way == 1 else 1
        return pltpu.make_async_remote_copy(
            src_ref=ref, dst_ref=ref, send_sem=z_send.at[i, side, k], recv_sem=z_recv.at[i, side, k],
            device_id=at_z(way), device_id_type=MESH,
        )

    def z_wait(i, way, k):
        source = lax.rem(z - way * k + NZ, NZ)
        ref = held.at[i, source]
        if k == NZ // 2:
            ref = ref.at[pl.ds(0 if way == 1 else STATIONS // 2, STATIONS // 2)]
        side = 0 if way == 1 else 1
        pltpu.make_async_copy(ref, ref, z_recv.at[i, side, k - 1]).wait()

    def t_copy(way, k):
        source = lax.rem(z - way * k + NZ, NZ)
        side = 0 if way == 1 else 1
        return pltpu.make_async_remote_copy(
            src_ref=table_all.at[source], dst_ref=table_all.at[source],
            send_sem=t_send.at[side, k], recv_sem=t_recv.at[side, k],
            device_id=at_z(way), device_id_type=MESH,
        )

    def t_wait(way, k):
        source = lax.rem(z - way * k + NZ, NZ)
        side = 0 if way == 1 else 1
        pltpu.make_async_copy(table_all.at[source], table_all.at[source], t_recv.at[side, k - 1]).wait()

    def to_smem(source):
        copy = pltpu.make_async_copy(table_all.at[source], table_smem.at[source], smem_sem)
        copy.start()
        copy.wait()

    def pick(i, source):
        for s in range(STATIONS):
            work[s] = held[i, source, s]
        place = source * YC + yc

        @pl.loop(0, YC)
        def _(step):
            to = lax.rem(yc + step, YC)
            for c in range(CAP):
                wanted = table_smem[source, z, to * CAP + c]
                stage[i, source, step, c] = work[wanted]

            @pl.when(step > 0)
            def _():
                pltpu.make_async_remote_copy(
                    src_ref=stage.at[i, source, step], dst_ref=landed.at[i, pl.ds(place * CAP, CAP)],
                    send_sem=y_send.at[i], recv_sem=y_recv.at[i],
                    device_id=at_yc(step), device_id_type=MESH,
                ).start()

        for c in range(CAP):
            landed[i, place * CAP + c] = stage[i, source, 0, c]

    half = NZ // 2
    for way in (1, -1):
        z_copy(0, way, 0).start()
        t_copy(way, 0).start()
    for step in (1, 3, 2):
        x_copy(step).start()
    to_smem(z)

    for t in range(NX + half):
        for i in range(NX):
            k = t - i
            if k < 0 or k > half:
                continue
            if k == 0:
                if i > 0:
                    pltpu.make_async_copy(quarters.at[0], held.at[i, z], x_recv.at[i - 1]).wait()
                    for way in (1, -1):
                        z_copy(i, way, 0).start()
            else:
                for way in (1, -1):
                    z_wait(i, way, k)
                    if k < half:
                        z_copy(i, way, k).start()
                if i == 0:
                    t_wait(1, k)
                    if k < half:
                        t_copy(1, k).start()
                        t_wait(-1, k)
                        if k < half - 1:
                            t_copy(-1, k).start()
        for i in range(NX):
            k = t - i
            if k < 0 or k > half:
                continue
            sources = [lax.rem(z - k + NZ, NZ)]
            if 0 < k < half:
                sources.append(lax.rem(z + k, NZ))
            for source in sources:
                if i == 0 and k > 0:
                    to_smem(source)
                pick(i, source)

    load_fine.wait()
    load_coarse.wait()

    @pl.loop(0, QUARTER // FINE)
    def _(j):
        cc = coarse[0, pl.ds(j, 1), :]
        sc = coarse[1, pl.ds(j, 1), :]
        rows = pl.ds(pl.multiple_of(j * FINE, FINE), FINE)
        later = pl.ds(pl.multiple_of(QUARTER + j * FINE, FINE), FINE)
        wave[rows, :] = (cc * fine[0] - sc * fine[1]).astype(jnp.bfloat16)
        wave[later, :] = (-(sc * fine[0] + cc * fine[1])).astype(jnp.bfloat16)

    sent = (RECV // YC) * (YC - 1)
    for i in range(NX):
        block = landed.at[i, pl.ds(0, sent)]
        pltpu.make_async_copy(block, block, y_recv.at[i]).wait()

        @pl.loop(0, RECV // 8)
        def _(g):
            for e in range(8):
                wide[g * 8 + e] = landed[i, g * 8 + e].astype(jnp.float32)

        @pl.loop(0, SLOTS // 8)
        def _(g):
            for e in range(8):
                p = g * 8 + e
                left = wide[pairs[p, 0]]
                right = wide[pairs[p, 1]]
                lre, lim = left[:ROWS], left[ROWS:]
                rre, rim = right[:ROWS], right[ROWS:]
                re = lre * rre + lim * rim
                im = lre * rim - lim * rre
                first = pl.ds(pl.multiple_of(p * 2 * ROWS, ROWS), ROWS)
                second = pl.ds(pl.multiple_of(p * 2 * ROWS + ROWS, ROWS), ROWS)
                if i == 0:
                    stack[first, :] = re
                    stack[second, :] = im
                else:
                    stack[first, :] += re
                    stack[second, :] += im

    for j in range(2 * ROWS):
        lhs[:, j * 128 : (j + 1) * 128] = stack[pl.ds(j, SLOTS, stride=2 * ROWS), :].astype(jnp.bfloat16)

    def r_copy(step, n):
        return pltpu.make_async_remote_copy(
            src_ref=parts_out.at[step - 1, n], dst_ref=parts_in.at[step - 1, n],
            send_sem=r_send.at[step - 1, n], recv_sem=r_recv.at[step - 1, n],
            device_id=at_x(step), device_id_type=MESH,
        )

    steps = LAGS // LAG_STEP
    for n in range(steps):
        columns = slice(n * LAG_STEP, (n + 1) * LAG_STEP)
        total[n] = jnp.dot(lhs[...], wave[:, columns], preferred_element_type=jnp.float32)
        for step in (2, 1, 3):
            rows = pl.ds(pl.multiple_of(lax.rem(win + step, NX) * SHARE, SHARE), SHARE)
            parts_out[step - 1, n] = total[n, rows, :].astype(jnp.bfloat16)
            r_copy(step, n).start()

    rows = pl.ds(pl.multiple_of(win * SHARE, SHARE), SHARE)
    live = win * SHARE + lax.broadcasted_iota(jnp.int32, (SHARE, LAG_STEP), 0) < counts[0]
    for n in range(steps):
        value = total[n, rows, :]
        for step in (1, 3, 2):
            r_copy(step, n).wait_recv()
            value = value + parts_in[step - 1, n].astype(jnp.float32)
        value = value * (1.0 / math.sqrt(WIDTH))
        out[:, n * LAG_STEP : (n + 1) * LAG_STEP] = jnp.where(live, value, 0.0)

    for step in (1, 2, 3):
        x_copy(step).wait_send()
        for n in range(steps):
            r_copy(step, n).wait_send()
    for i in range(NX):
        block = landed.at[i, pl.ds(0, sent)]
        pltpu.make_async_copy(block, block, y_send.at[i]).wait()
        for way in (1, -1):
            for k in range(half):
                z_copy(i, way, k).wait_send()
    for k in range(half):
        t_copy(1, k).wait_send()
        if k < half - 1:
            t_copy(-1, k).wait_send()


def local(spectra, wanted, pairs, counts):
    table = jnp.pad(wanted.reshape(NZ, YC * CAP), ((0, 0), (0, 128 - YC * CAP)))
    fine, coarse = tables()
    vmem = pl.BlockSpec(memory_space=pltpu.VMEM)
    smem = pl.BlockSpec(memory_space=pltpu.SMEM)
    anywhere = pl.BlockSpec(memory_space=pl.ANY)
    half = NZ // 2
    steps = LAGS // LAG_STEP
    bf16, f32 = jnp.bfloat16, jnp.float32
    dma = pltpu.SemaphoreType.DMA
    return pl.pallas_call(
        kernel,
        out_shape=jax.ShapeDtypeStruct((SHARE, LAGS), f32),
        in_specs=[vmem, vmem, smem, smem, anywhere, anywhere],
        out_specs=vmem,
        scratch_shapes=[
            pltpu.VMEM((STATIONS * 2 * (WIDTH // 128), 128), f32),
            pltpu.VMEM((NX - 1, STATIONS, 2 * ROWS, 128), bf16),
            pltpu.VMEM((NX, NZ, STATIONS, 2 * ROWS, 128), bf16),
            pltpu.VMEM((STATIONS, 2 * ROWS, 128), bf16),
            pltpu.VMEM((NX, NZ, YC, CAP, 2 * ROWS, 128), bf16),
            pltpu.VMEM((NX, RECV, 2 * ROWS, 128), bf16),
            pltpu.VMEM((RECV, 2 * ROWS, 128), f32),
            pltpu.VMEM((SLOTS * 2 * ROWS, 128), f32),
            pltpu.VMEM((SLOTS, 2 * QUARTER), bf16),
            pltpu.VMEM((2 * QUARTER, LAGS), bf16),
            pltpu.VMEM((steps, SLOTS, LAG_STEP), f32),
            pltpu.VMEM((NX - 1, steps, SHARE, LAG_STEP), bf16),
            pltpu.VMEM((NX - 1, steps, SHARE, LAG_STEP), bf16),
            pltpu.VMEM((NZ, 8, 128), jnp.int32),
            pltpu.SMEM((NZ, 8, 128), jnp.int32),
            pltpu.VMEM((2, FINE, LAGS), f32),
            pltpu.VMEM((2, QUARTER // FINE, LAGS), f32),
            dma((NX - 1,)), dma((NX - 1,)),
            dma((NX, 2, half)), dma((NX, 2, half)),
            dma((2, half)), dma((2, half)),
            dma((NX,)), dma((NX,)),
            dma((NX - 1, steps)), dma((NX - 1, steps)),
            dma((2,)), dma,
        ],
        compiler_params=pltpu.CompilerParams(
            collective_id=0, has_side_effects=True, vmem_limit_bytes=48 << 20
        ),
        name="correlate",
    )(spectra[0], table, pairs, counts, fine, coarse)


def solution(mesh):
    placed = (P("win", "sta", None), P("sta", None, None), P("sta", None), P("sta"))
    return jax.shard_map(
        local, mesh=mesh, in_specs=placed, out_specs=P(("sta", "win"), None), check_vma=False
    )
```

time: 269 us -> 69.6 us (0.26)
  waiting for transfers between devices: 114 us -> 0 us
  Pallas kernels: 0 us -> 63.7 us
  other arithmetic: 61.4 us -> 0 us
  local copies, waits for them, and re-layouts: 50.2 us -> 4.92 us
  starting transfers between devices: 19 us -> 0 us
  between operations: 14.3 us -> 0.7 us
  matrix products: 8.28 us -> 0 us
    all_to_all x2 -> x0, waiting for transfers between devices: 94 us -> none  [the longest x1 88.8 us: local(): lax.all_to_all(outgoing, 'sta', split_axis=0, concat_axis=0, tiled=True)]
    pallas_call x0 -> x1, Pallas kernels: none -> 63.7 us  [local(): pl.pallas_call(kernel, out_shape=jax.ShapeDtypeStruct((SHARE, LAGS), f32)...]
    reduce_sum x2 -> x0, other arithmetic: 34.8 us -> none  [the longest x1 34.6 us: local(): stack_re = jnp.sum(lre * rre + lim * rim, axis=1)]
    convert_element_type x2 -> x0, local copies, waits for them, and re-layouts: 23.5 us -> none  [the longest x1 11.8 us: local(): jnp.take(received, pairs[:, 0], axis=0).reshape(-1, parts, 2, quarter)]
    reduce_scatter x1 -> x0, waiting for transfers between devices: 20.1 us -> none  [local(): lax.psum_scatter(partial, 'win', scatter_dimension=0, tiled=True)]
    all_to_all x2 -> x0, starting transfers between devices: 18.9 us -> none  [the longest x1 14.1 us: local(): lax.all_to_all(outgoing, 'sta', split_axis=0, concat_axis=0, tiled=True)]
    gather x4 -> x0, local copies, waits for them, and re-layouts: 17.3 us -> none  [the longest x2 6.96 us: local(): outgoing = jnp.take(mixed, wanted[0].reshape(-1), axis=0)]
    convert_element_type x3 -> x0, other arithmetic: 13.1 us -> none  [the longest x1 6.01 us: local(): jnp.take(received, pairs[:, 0], axis=0).reshape(-1, parts, 2, quarter)]
  transfers between devices with their start and end apart: 3 -> 0, of which waited for: 3 -> 0; matrix products, arithmetic and copies ran while one was open for 2% -> 0% of each run, Pallas kernels for 0% -> 0%
where the time goes in v2:
time: 69.6 us; the launch traced here: 69.4 us
  Pallas kernels  63.7 us (92%)
  local copies, waits for them, and re-layouts  4.92 us (7%)
  between operations  0.7 us (1%)
    pallas_call x1, Pallas kernels, local(): pl.pallas_call(kernel, out_shape=jax.ShapeDtypeStruct((SHARE, LAGS), f32)...  63.7 us
    unnamed x13, local copies, waits for them, and re-layouts  4.84 us

profile of v2, /device:TPU:1, one launch (start us, length us, event | category | flops | bytes accessed | tf_op | source)
XLA Modules:
  0.0 69.4 jit_solution(9415321308311016324)
XLA Ops:
  0.0 0.0 copy-start.4
  0.7 0.0 copy-done.4
  0.7 0.1 copy.9
  0.8 0.1 reshape.3
  0.9 0.0 copy-start.3
  0.9 0.7 copy-done.3
  1.5 0.1 copy.10.pairs
  1.7 0.0 copy-start
  1.7 1.2 %copy-done = f32[2,128,1024]{2,1,0:T(8,128)S(1)} copy-done((f32[2,128,1024]{2,1,0:T(8,128)S(1)}, f32[2,128,1024]{2,1,0:T(8,128)}, u32[]{:S(2)}) %copy-start) | copy-done | bytes 1048600
  2.9 0.0 copy-start.1
  2.9 1.0 %copy-done.1 = f32[1,16,8192]{2,1,0:T(8,128)S(1)} copy-done((f32[1,16,8192]{2,1,0:T(8,128)S(1)}, f32[1,16,8192]{2,1,0:T(8,128)}, u32[]{:S(2)}) %copy-start.1) | copy-done | bytes 524312
  4.0 0.0 copy-start.2
  4.0 0.9 %copy-done.2 = f32[2,32,1024]{2,1,0:T(8,128)S(1)} copy-done((f32[2,32,1024]{2,1,0:T(8,128)S(1)}, f32[2,32,1024]{2,1,0:T(8,128)}, u32[]{:S(2)}) %copy-start.2) | copy-done | bytes 262168
  4.9 63.7 %correlate.1 = f32[64,1024]{1,0:T(8,128)S(1)} custom-call(f32[16,8192]{1,0:T(8,128)S(1)} %bitcast.1, s32[8,128]{1,0:T(8,128)S(1)} %pad.4.table, s32[256,2]{1,0:T(8,128)S(1)} %copy.10.pairs, s32[1]{0:T(128)S(6)} %copy.12.counts, f32[2,32,1024]{2,1,0:T(8,128)S(1)} %copy-done.2, f32[2,128,1024]{2,1,0:T(8,128)S(1)} %copy-done), custom_call_target="tpu_custom_call" | custom-call | tf_op jit(solution)/shard_map/correlate/pallas_call | solution.py:315
  68.7 0.7 %copy.13 = f32[64,1024]{1,0:T(8,128)} copy(f32[64,1024]{1,0:T(8,128)S(1)} %correlate.1) | data formatting | bytes 524288
  (1 shorter events, 0.0 us)
Async XLA Ops:
  0.0 0.7 copy-start.4
  0.9 0.7 copy-start.3
  1.7 1.2 %copy-start = (f32[2,128,1024]{2,1,0:T(8,128)S(1)}, f32[2,128,1024]{2,1,0:T(8,128)}, u32[]{:S(2)}) copy-start(f32[2,128,1024]{2,1,0:T(8,128)} %constant.7.clone.coarse_hbm) | copy-start | bytes 3145732
  2.9 1.0 %copy-start.1 = (f32[1,16,8192]{2,1,0:T(8,128)S(1)}, f32[1,16,8192]{2,1,0:T(8,128)}, u32[]{:S(2)}) copy-start(f32[1,16,8192]{2,1,0:T(8,128)} %param.6) | copy-start | bytes 1572868
  4.0 0.9 %copy-start.2 = (f32[2,32,1024]{2,1,0:T(8,128)S(1)}, f32[2,32,1024]{2,1,0:T(8,128)}, u32[]{:S(2)}) copy-start(f32[2,32,1024]{2,1,0:T(8,128)} %constant.6.clone.fine_hbm) | copy-start | bytes 786436

commit v3 on v2

v3 whole, which is shorter than its diff:
```python
import functools
import math

import jax
import jax.numpy as jnp
import numpy as np
from jax import lax
from jax.experimental import pallas as pl
from jax.experimental.pallas import tpu as pltpu
from jax.sharding import PartitionSpec as P

BAND = 64
LAGS = 1024
FINE = 32
NZ, NY, NC, NX = 8, 4, 2, 4
YC = NY * NC
STATIONS = 16
CAP = 3
WIDTH = 4096
QUARTER = WIDTH // NX
ROWS = QUARTER // 128
SLOTS = 256
SHARE = SLOTS // NX
RECV = NZ * YC * CAP
LAG_STEP = 256
SHIFT = (0, 1, 3, 2)
FAR = (0, 1)
REACH = 3
NEAR = 1 + 2 * REACH
ORDER = (
    "x0", "p00", "z01", "p01", "x1", "p10", "x2", "p20", "z02", "x3", "p30", "w0",
    "p02", "z11", "p11", "z21", "p21", "z31", "p31", "w1", "z03", "z12", "p03", "z22",
    "p22", "p12", "z04", "z32", "p04", "w2", "z13", "z23", "p13", "p23", "z33", "z14",
    "f0", "z24", "z34", "p14", "p24", "w3", "p33", "p32", "f1", "p34", "c0", "c2",
    "c1", "c3",
)
FIRST_FAR = [int(event[1]) for event in ORDER if event[0] == "f"][:1]
FIRST_CROSS = [int(event[1]) for event in ORDER if event[0] == "c"][:1]
WAVE_STEPS = 4
MESH = pl.DeviceIdType.MESH


def tables():
    lag = np.arange(LAGS, dtype=np.int64) - LAGS // 2
    period = 2 * WIDTH

    def both(freq):
        angle = (freq[:, None] * lag[None, :]) % period * (2.0 * np.pi / period)
        return np.stack([np.cos(angle), np.sin(angle)]).astype(np.float32)

    return both(np.arange(FINE)), both(np.arange(0, WIDTH, FINE))


def kernel(
    spectra_hbm, table_hbm, pairs_hbm, counts, fine_hbm, coarse_hbm, out,
    spectra, pairs, terms, sums, white32, quarters, held, work, stage, landed, wide, stack, lhs, wave, total, half_out, half_in, parts_out, parts_in,
    table_all, table_smem, fine, coarse,
    far, stage_far, table_far, table_far_smem, f_send, f_recv,
    x_send, x_recv, z_send, z_recv, t_send, t_recv, y_send, y_recv, h_send, h_recv, r_send, r_recv, local_sem, smem_sem,
):
    win = lax.axis_index("win")
    sta = lax.axis_index("sta")
    z = sta // YC
    yc = lax.rem(sta, YC)
    y = yc // NC
    core = lax.rem(yc, NC)
    across = lax.rem(y + NY // 2, NY) * NC + core

    def at_x(step):
        return (sta, lax.rem(win + step, NX))

    def at_z(step):
        return (lax.rem(z + step + NZ, NZ) * YC + yc, win)

    def at_yc(step):
        to = lax.rem(y + step // NC, NY) * NC + lax.rem(core + lax.rem(step, NC), NC)
        return to, (z * YC + to, win)

    def at_zc(step):
        along = step // NC
        along = along + jnp.where(along > REACH, NZ - NEAR, 0)
        to = lax.rem(z + along, NZ) * YC + y * NC + lax.rem(core + lax.rem(step, NC), NC)
        return to, (to, win)

    def to_smem(source):
        return pltpu.make_async_copy(table_all.at[source], table_smem.at[source], smem_sem.at[source])

    def far_to_smem():
        return pltpu.make_async_copy(table_far, table_far_smem, smem_sem.at[NZ])

    barrier = pltpu.get_barrier_semaphore()
    for step in (1, 2, 3):
        pl.semaphore_signal(barrier, inc=1, device_id=at_x(step), device_id_type=MESH)
    for step in range(1, YC):
        pl.semaphore_signal(barrier, inc=1, device_id=at_yc(step)[1], device_id_type=MESH)
    for step in range(NC, NEAR * NC):
        pl.semaphore_signal(barrier, inc=1, device_id=at_zc(step)[1], device_id_type=MESH)

    load_spectra = pltpu.make_async_copy(spectra_hbm, spectra, local_sem.at[2])
    load_spectra.start()
    load_table = pltpu.make_async_copy(table_hbm, table_all.at[z], local_sem.at[3])
    load_table.start()
    load_pairs = pltpu.make_async_copy(pairs_hbm, pairs, local_sem.at[4])
    load_pairs.start()
    load_fine = pltpu.make_async_copy(fine_hbm, fine, local_sem.at[0])
    load_fine.start()
    own_coarse = coarse_hbm.at[:, pl.ds(pl.multiple_of(win * FINE, FINE), FINE)]
    load_coarse = pltpu.make_async_copy(own_coarse, coarse, local_sem.at[1])
    load_coarse.start()

    lane_r = lax.rem(lax.broadcasted_iota(jnp.int32, (3 * 128, 128), 0), 128) // BAND
    lane_c = lax.broadcasted_iota(jnp.int32, (3 * 128, 128), 1) // BAND
    same = jnp.where(lane_r == lane_c, 1.0, 0.0).astype(jnp.bfloat16)
    chunks = WIDTH // 128
    load_spectra.wait()

    for j in range(chunks):
        re = spectra[:, j * 128 : (j + 1) * 128]
        im = spectra[:, WIDTH + j * 128 : WIDTH + (j + 1) * 128]
        rest = jnp.sqrt(re * re + im * im)
        for term in range(3):
            rounded = rest.astype(jnp.bfloat16)
            terms[j * STATIONS : (j + 1) * STATIONS, term * 128 : (term + 1) * 128] = rounded
            rest = rest - rounded.astype(jnp.float32)
    sums[...] = jnp.dot(terms[...], same, preferred_element_type=jnp.float32)
    for j in range(chunks):
        band = sums[j * STATIONS : (j + 1) * STATIONS, :] * (1.0 / BAND) + 1e-06
        inverse = 1.0 / band
        re = spectra[:, j * 128 : (j + 1) * 128]
        im = spectra[:, WIDTH + j * 128 : WIDTH + (j + 1) * 128]
        white32[pl.ds(j, STATIONS, stride=2 * chunks), :] = re * inverse
        white32[pl.ds(chunks + j, STATIONS, stride=2 * chunks), :] = im * inverse

    @pl.loop(0, STATIONS)
    def _(s):
        for step in range(NX):
            quarter = lax.rem(win + step, NX)
            base = s * 2 * chunks + quarter * ROWS
            re = white32[pl.ds(pl.multiple_of(base, ROWS), ROWS), :]
            im = white32[pl.ds(pl.multiple_of(base + chunks, ROWS), ROWS), :]
            slab = jnp.concatenate([re, im], axis=0).astype(jnp.bfloat16)
            if step == 0:
                held[0, z, s] = slab
            else:
                quarters[step - 1, s] = slab

    load_table.wait()
    to_smem(z).start()
    load_pairs.wait()
    pl.semaphore_wait(barrier, 3 + YC - 1 + NEAR * NC - NC)

    def x_copy(step):
        place = SHIFT.index((NX - step) % NX)
        return pltpu.make_async_remote_copy(
            src_ref=quarters.at[step - 1], dst_ref=held.at[place, z],
            send_sem=x_send.at[place - 1], recv_sem=x_recv.at[place - 1],
            device_id=at_x(step), device_id_type=MESH,
        )

    def z_copy(i, way, k):
        source = lax.rem(z - way * k + NZ, NZ)
        ref = held.at[i, source]
        if k == NZ // 2 - 1:
            ref = ref.at[pl.ds(0 if way == 1 else STATIONS // 2, STATIONS // 2)]
        side = 0 if way == 1 else 1
        return pltpu.make_async_remote_copy(
            src_ref=ref, dst_ref=ref, send_sem=z_send.at[i, side, k], recv_sem=z_recv.at[i, side, k],
            device_id=at_z(way), device_id_type=MESH,
        )

    def z_wait(i, way, k):
        source = lax.rem(z - way * k + NZ, NZ)
        ref = held.at[i, source]
        if k == NZ // 2:
            ref = ref.at[pl.ds(0 if way == 1 else STATIONS // 2, STATIONS // 2)]
        side = 0 if way == 1 else 1
        pltpu.make_async_copy(ref, ref, z_recv.at[i, side, k - 1]).wait()

    def t_copy(way, k):
        source = lax.rem(z - way * k + NZ, NZ)
        side = 0 if way == 1 else 1
        return pltpu.make_async_remote_copy(
            src_ref=table_all.at[source], dst_ref=table_all.at[source],
            send_sem=t_send.at[side, k], recv_sem=t_recv.at[side, k],
            device_id=at_z(way), device_id_type=MESH,
        )

    def t_wait(way, k):
        source = lax.rem(z - way * k + NZ, NZ)
        side = 0 if way == 1 else 1
        pltpu.make_async_copy(table_all.at[source], table_all.at[source], t_recv.at[side, k - 1]).wait()

    def far_copy(i):
        return pltpu.make_async_remote_copy(
            src_ref=held.at[i, z], dst_ref=far.at[FAR.index(i)],
            send_sem=f_send.at[FAR.index(i)], recv_sem=f_recv.at[FAR.index(i)],
            device_id=(z * YC + across, win), device_id_type=MESH,
        )

    def far_table_copy():
        return pltpu.make_async_remote_copy(
            src_ref=table_all.at[z], dst_ref=table_far,
            send_sem=f_send.at[len(FAR)], recv_sem=f_recv.at[len(FAR)],
            device_id=(z * YC + across, win), device_id_type=MESH,
        )

    def pick(i, source, k):
        for s in range(STATIONS):
            work[s] = held[i, source, s]
        place = source * YC + yc

        skip = i in FAR and k <= REACH

        @pl.loop(0, YC - NC if skip else YC)
        def _(turn):
            step = turn
            if skip:
                step = turn + jnp.where(turn >= YC // 2, NC, 0)
            to, device = at_yc(step)
            for c in range(CAP):
                wanted = table_smem[source, c, 0, z * YC + to]
                stage[i, source, step, c] = work[wanted]

            @pl.when(step > 0)
            def _():
                pltpu.make_async_remote_copy(
                    src_ref=stage.at[i, source, step], dst_ref=landed.at[i, pl.ds(place * CAP, CAP)],
                    send_sem=y_send.at[i], recv_sem=y_recv.at[i],
                    device_id=device, device_id_type=MESH,
                ).start()

        for c in range(CAP):
            landed[i, place * CAP + c] = stage[i, source, 0, c]

    def pick_far(i):
        at = FAR.index(i)
        if [i] == FIRST_FAR:
            far_table_copy().wait_recv()
            far_to_smem().start()
            far_to_smem().wait()
        far_copy(i).wait_recv()
        for s in range(STATIONS):
            work[s] = far[at, s]
        place = z * YC + across

        @pl.loop(0, NEAR * NC)
        def _(step):
            to, device = at_zc(step)
            for c in range(CAP):
                stage_far[at, step, c] = work[table_far_smem[c, 0, to]]

            @pl.when(step > 0)
            def _():
                pltpu.make_async_remote_copy(
                    src_ref=stage_far.at[at, step], dst_ref=landed.at[i, pl.ds(place * CAP, CAP)],
                    send_sem=y_send.at[i], recv_sem=y_recv.at[i],
                    device_id=device, device_id_type=MESH,
                ).start()

        for c in range(CAP):
            landed[i, place * CAP + c] = stage_far[at, 0, c]

    def make_wave(step):
        count = QUARTER // FINE // WAVE_STEPS

        @pl.loop(step * count, (step + 1) * count)
        def _(j):
            cc = coarse[0, pl.ds(j, 1), :]
            sc = coarse[1, pl.ds(j, 1), :]
            rows = pl.ds(pl.multiple_of(j * FINE, FINE), FINE)
            later = pl.ds(pl.multiple_of(QUARTER + j * FINE, FINE), FINE)
            wave[rows, :] = (cc * fine[0] - sc * fine[1]).astype(jnp.bfloat16)
            wave[later, :] = (-(sc * fine[0] + cc * fine[1])).astype(jnp.bfloat16)

    half = NZ // 2
    for step in (1, 3, 2):
        x_copy(step).start()
    for way in (1, -1):
        z_copy(0, way, 0).start()
        t_copy(way, 0).start()
    if 0 in FAR:
        far_copy(0).start()
    if FAR:
        far_table_copy().start()

    def sent(i):
        direct = NZ * (YC - 1)
        return CAP * (direct - NEAR * NC + NEAR * NC - 1 if i in FAR else direct)

    def cross(i):
        arrived = landed.at[i, pl.ds(0, sent(i))]
        pltpu.make_async_copy(arrived, arrived, y_recv.at[i]).wait()

        @pl.loop(0, RECV // 8)
        def _(g):
            for e in range(8):
                wide[g * 8 + e] = landed[i, g * 8 + e].astype(jnp.float32)

        @pl.loop(0, SLOTS // 8)
        def _(g):
            for e in range(8):
                p = g * 8 + e
                left = wide[pairs[0, p]]
                right = wide[pairs[1, p]]
                lre, lim = left[:ROWS], left[ROWS:]
                rre, rim = right[:ROWS], right[ROWS:]
                re = lre * rre + lim * rim
                im = lre * rim - lim * rre
                first = pl.ds(pl.multiple_of(p * 2 * ROWS, ROWS), ROWS)
                second = pl.ds(pl.multiple_of(p * 2 * ROWS + ROWS, ROWS), ROWS)
                if [i] == FIRST_CROSS:
                    stack[first, :] = re
                    stack[second, :] = im
                else:
                    stack[first, :] += re
                    stack[second, :] += im

    for event in ORDER:
        kind, i = event[0], int(event[1])
        k = int(event[2]) if len(event) > 2 else 0
        if kind == "x" and i > 0:
            pltpu.make_async_copy(quarters.at[0], held.at[i, z], x_recv.at[i - 1]).wait()
            for way in (1, -1):
                z_copy(i, way, 0).start()
            if i in FAR:
                far_copy(i).start()
        elif kind == "z":
            for way in (1, -1):
                z_wait(i, way, k)
                if k < half:
                    z_copy(i, way, k).start()
            if i == 0:
                t_wait(1, k)
                to_smem(lax.rem(z - k + NZ, NZ)).start()
                if k < half:
                    t_copy(1, k).start()
                    t_wait(-1, k)
                    to_smem(lax.rem(z + k, NZ)).start()
                    if k < half - 1:
                        t_copy(-1, k).start()
        elif kind == "p":
            sources = [lax.rem(z - k + NZ, NZ)]
            if 0 < k < half:
                sources.append(lax.rem(z + k, NZ))
            for source in sources:
                if i == 0:
                    to_smem(source).wait()
                pick(i, source, k)
        elif kind == "f":
            pick_far(i)
        elif kind == "c":
            cross(i)
        elif kind == "w":
            if i == 0:
                load_fine.wait()
                load_coarse.wait()
            make_wave(i)

    for j in range(2 * ROWS):
        lhs[:, j * 128 : (j + 1) * 128] = stack[pl.ds(j, SLOTS, stride=2 * ROWS), :].astype(jnp.bfloat16)

    sides = ((0, 1), (1, NX - 1))
    part = SHARE // 2

    def h_copy(side, step, n):
        return pltpu.make_async_remote_copy(
            src_ref=half_out.at[side, n], dst_ref=half_in.at[side, n],
            send_sem=h_send.at[side, n], recv_sem=h_recv.at[side, n],
            device_id=at_x(step), device_id_type=MESH,
        )

    def r_copy(side, step, n, late):
        first = side * part if late else (1 - side) * part
        return pltpu.make_async_remote_copy(
            src_ref=parts_out.at[side, n, pl.ds(first, part)], dst_ref=parts_in.at[side, n, pl.ds(first, part)],
            send_sem=r_send.at[side, n, int(late)], recv_sem=r_recv.at[side, n, int(late)],
            device_id=at_x(step), device_id_type=MESH,
        )

    def block(n, step, first, count):
        base = lax.rem(win + step, NX) * SHARE + first
        return total[n, pl.ds(pl.multiple_of(base, count), count), :]

    steps = LAGS // LAG_STEP
    for n in range(steps):
        columns = slice(n * LAG_STEP, (n + 1) * LAG_STEP)
        total[n] = jnp.dot(lhs[...], wave[:, columns], preferred_element_type=jnp.float32)
        for side, step in sides:
            half_out[side, n] = block(n, 2, side * part, part).astype(jnp.bfloat16)
            h_copy(side, step, n).start()
    for n in range(steps):
        for side, step in sides:
            first = (1 - side) * part
            parts_out[side, n, first : first + part] = block(n, step, first, part).astype(jnp.bfloat16)
            r_copy(side, step, n, False).start()
    for n in range(steps):
        for side, step in sides:
            first = side * part
            h_copy(side, step, n).wait_recv()
            value = block(n, step, first, part) + half_in[side, n].astype(jnp.float32)
            parts_out[side, n, first : first + part] = value.astype(jnp.bfloat16)
            r_copy(side, step, n, True).start()

    live = win * SHARE + lax.broadcasted_iota(jnp.int32, (SHARE, LAG_STEP), 0) < counts[0]
    for n in range(steps):
        value = block(n, 0, 0, SHARE)
        for side, step in sides:
            for late in (False, True):
                r_copy(side, step, n, late).wait_recv()
            value = value + parts_in[side, n].astype(jnp.float32)
        value = value * (1.0 / math.sqrt(WIDTH))
        out[:, n * LAG_STEP : (n + 1) * LAG_STEP] = jnp.where(live, value, 0.0)

    for step in (1, 2, 3):
        x_copy(step).wait_send()
    for side, step in sides:
        for n in range(steps):
            h_copy(side, step, n).wait_send()
            for late in (False, True):
                r_copy(side, step, n, late).wait_send()
    for i in range(NX):
        arrived = landed.at[i, pl.ds(0, sent(i))]
        pltpu.make_async_copy(arrived, arrived, y_send.at[i]).wait()
        for way in (1, -1):
            for k in range(half):
                z_copy(i, way, k).wait_send()
    if FAR:
        far_table_copy().wait_send()
    for i in FAR:
        far_copy(i).wait_send()
    for k in range(half):
        t_copy(1, k).wait_send()
        if k < half - 1:
            t_copy(-1, k).wait_send()


def local(spectra, wanted, pairs, counts):
    table = jnp.transpose(wanted, (2, 0, 1))
    fine, coarse = tables()
    vmem = pl.BlockSpec(memory_space=pltpu.VMEM)
    smem = pl.BlockSpec(memory_space=pltpu.SMEM)
    hbm = pl.BlockSpec(memory_space=pltpu.HBM)
    half = NZ // 2
    steps = LAGS // LAG_STEP
    bf16, f32 = jnp.bfloat16, jnp.float32
    dma = pltpu.SemaphoreType.DMA
    held_in_hbm = [
        pltpu.with_memory_space_constraint(jnp.asarray(x), pltpu.HBM) for x in (spectra[0], table, pairs.T, fine, coarse)
    ]
    return pl.pallas_call(
        kernel,
        out_shape=jax.ShapeDtypeStruct((SHARE, LAGS), f32),
        in_specs=[hbm, hbm, hbm, smem, hbm, hbm],
        out_specs=vmem,
        scratch_shapes=[
            pltpu.VMEM((STATIONS, 2 * WIDTH), f32),
            pltpu.SMEM((2, SLOTS), jnp.int32),
            pltpu.VMEM((STATIONS * WIDTH // 128, 3 * 128), bf16),
            pltpu.VMEM((STATIONS * WIDTH // 128, 128), f32),
            pltpu.VMEM((STATIONS * 2 * (WIDTH // 128), 128), f32),
            pltpu.VMEM((NX - 1, STATIONS, 2 * ROWS, 128), bf16),
            pltpu.VMEM((NX, NZ, STATIONS, 2 * ROWS, 128), bf16),
            pltpu.VMEM((STATIONS, 2 * ROWS, 128), bf16),
            pltpu.VMEM((NX, NZ, YC, CAP, 2 * ROWS, 128), bf16),
            pltpu.VMEM((NX, RECV, 2 * ROWS, 128), bf16),
            pltpu.VMEM((RECV, 2 * ROWS, 128), f32),
            pltpu.VMEM((SLOTS * 2 * ROWS, 128), f32),
            pltpu.VMEM((SLOTS, 2 * QUARTER), bf16),
            pltpu.VMEM((2 * QUARTER, LAGS), bf16),
            pltpu.VMEM((steps, SLOTS, LAG_STEP), f32),
            pltpu.VMEM((2, steps, SHARE // 2, LAG_STEP), bf16),
            pltpu.VMEM((2, steps, SHARE // 2, LAG_STEP), bf16),
            pltpu.VMEM((2, steps, SHARE, LAG_STEP), bf16),
            pltpu.VMEM((2, steps, SHARE, LAG_STEP), bf16),
            pltpu.VMEM((NZ, CAP, 1, NZ * YC), jnp.int32),
            pltpu.SMEM((NZ, CAP, 1, NZ * YC), jnp.int32),
            pltpu.VMEM((2, FINE, LAGS), f32),
            pltpu.VMEM((2, QUARTER // FINE, LAGS), f32),
            pltpu.VMEM((max(len(FAR), 1), STATIONS, 2 * ROWS, 128), bf16),
            pltpu.VMEM((max(len(FAR), 1), NEAR * NC, CAP, 2 * ROWS, 128), bf16),
            pltpu.VMEM((CAP, 1, NZ * YC), jnp.int32),
            pltpu.SMEM((CAP, 1, NZ * YC), jnp.int32),
            dma((len(FAR) + 1,)), dma((len(FAR) + 1,)),
            dma((NX - 1,)), dma((NX - 1,)),
            dma((NX, 2, half)), dma((NX, 2, half)),
            dma((2, half)), dma((2, half)),
            dma((NX,)), dma((NX,)),
            dma((2, steps)), dma((2, steps)),
            dma((2, steps, 2)), dma((2, steps, 2)),
            dma((5,)), dma((NZ + 1,)),
        ],
        compiler_params=pltpu.CompilerParams(
            collective_id=0, has_side_effects=True, vmem_limit_bytes=48 << 20
        ),
        name="correlate",
    )(*held_in_hbm[:3], counts, *held_in_hbm[3:])


def solution(mesh):
    placed = (P("win", "sta", None), P("sta", None, None), P("sta", None), P("sta"))
    return jax.shard_map(
        local, mesh=mesh, in_specs=placed, out_specs=P(("sta", "win"), None), check_vma=False
    )
```

time: 69.6 us -> 57.3 us (0.82)
  Pallas kernels: 63.7 us -> 55.9 us
  local copies, waits for them, and re-layouts: 4.92 us -> 0.71 us
    pallas_call x1, Pallas kernels: 63.7 us -> 55.9 us  [local(): pl.pallas_call(kernel, out_shape=jax.ShapeDtypeStruct((SHARE, LAGS), f32)...]
    unnamed x13 -> x1, local copies, waits for them, and re-layouts: 4.84 us -> 0.71 us
where the time goes in v3:
time: 57.3 us; the launch traced here: 57.2 us
  Pallas kernels  55.9 us (98%)
  local copies, waits for them, and re-layouts  0.71 us (1%)
  between operations  0.66 us (1%)
    pallas_call x1, Pallas kernels, local(): pl.pallas_call(kernel, out_shape=jax.ShapeDtypeStruct((SHARE, LAGS), f32)...  55.9 us

profile of v3, /device:TPU:1, one launch (start us, length us, event | category | flops | bytes accessed | tf_op | source)
XLA Modules:
  0.0 57.2 jit_solution(1244856877368978699)
XLA Ops:
  0.7 55.9 %correlate.1 = f32[64,1024]{1,0:T(8,128)S(1)} custom-call(f32[16,8192]{1,0:T(8,128)} %bitcast.3, s32[3,1,64]{2,1,0:T(1,128)} %bitcast.5, s32[2,256]{1,0:T(2,128)} %bitcast.4, s32[1]{0:T(128)S(6)} %copy.8.counts, f32[2,32,1024]{2,1,0:T(8,128)} %constant.4.clone.fine_hbm, f32[2,128,1024]{2,1,0:T(8,128)} %constant.5.clone.coarse_hbm), custom_call_target="tpu_custom_call" | custom-call | tf_op jit(solution)/shard_map/correlate/pallas_call | solution.py:450
  56.5 0.7 %copy.9 = f32[64,1024]{1,0:T(8,128)} copy(f32[64,1024]{1,0:T(8,128)S(1)} %correlate.1) | data formatting | bytes 524288

commit v4 on v3

--- a/solution.py
+++ b/solution.py
@@ -1,5 +1,4 @@
 import functools
-import math
 
 import jax
 import jax.numpy as jnp
@@ -11,7 +10,6 @@
 
 BAND = 64
 LAGS = 1024
-FINE = 32
 NZ, NY, NC, NX = 8, 4, 2, 4
 YC = NY * NC
 STATIONS = 16
@@ -22,41 +20,65 @@
 SLOTS = 256
 SHARE = SLOTS // NX
 RECV = NZ * YC * CAP
-LAG_STEP = 256
+TERMS = 256
 SHIFT = (0, 1, 3, 2)
 FAR = (0, 1)
 REACH = 3
 NEAR = 1 + 2 * REACH
 ORDER = (
-    "x0", "p00", "z01", "p01", "x1", "p10", "x2", "p20", "z02", "x3", "p30", "w0",
-    "p02", "z11", "p11", "z21", "p21", "z31", "p31", "w1", "z03", "z12", "p03", "z22",
-    "p22", "p12", "z04", "z32", "p04", "w2", "z13", "z23", "p13", "p23", "z33", "z14",
-    "f0", "z24", "z34", "p14", "p24", "w3", "p33", "p32", "f1", "p34", "c0", "c2",
+    "x0", "p00", "z01", "p01", "x1", "p10", "x2", "p20", "z02", "x3", "p30",
+    "p02", "z11", "p11", "z21", "p21", "z31", "p31", "z03", "z12", "p03", "z22",
+    "p22", "p12", "z04", "z32", "p04", "z13", "z23", "p13", "p23", "z33", "z14",
+    "f0", "z24", "z34", "p14", "p24", "p33", "p32", "f1", "p34", "c0", "c2",
     "c1", "c3",
 )
 FIRST_FAR = [int(event[1]) for event in ORDER if event[0] == "f"][:1]
 FIRST_CROSS = [int(event[1]) for event in ORDER if event[0] == "c"][:1]
-WAVE_STEPS = 4
 MESH = pl.DeviceIdType.MESH
 
 
-def tables():
-    lag = np.arange(LAGS, dtype=np.int64) - LAGS // 2
-    period = 2 * WIDTH
-
-    def both(freq):
-        angle = (freq[:, None] * lag[None, :]) % period * (2.0 * np.pi / period)
-        return np.stack([np.cos(angle), np.sin(angle)]).astype(np.float32)
-
-    return both(np.arange(FINE)), both(np.arange(0, WIDTH, FINE))
+def bessel(x, count):
+    top = count + 160
+    f = np.zeros((top + 1,) + x.shape)
+    f[top - 1] = 1e-200
+    for n in range(top - 1, 0, -1):
+        f[n - 1] = (2 * n + 1) / x * f[n] - f[n + 1]
+        f[n - 1 :] *= np.where(np.abs(f[n - 1]) > 1e100, 1e-200, 1.0)
+    order = np.arange(top + 1)[:, None]
+    size = np.sqrt(np.sum((2 * order + 1) * f * f, axis=0))
+    first = np.sin(x) / x
+    second = (first - np.cos(x)) / x
+    return f[:count] * np.sign(f[0] * first + f[1] * second) / size
+
+
+def expansion():
+    offset = np.arange(QUARTER) - (QUARTER - 1) / 2
+    reach = (LAGS - 1) / 2
+    x = 2 * np.pi * offset * reach / (2 * WIDTH)
+    order = np.arange(TERMS)
+    j = bessel(np.abs(x), TERMS).T * np.where(x[:, None] < 0, (-1.0) ** order, 1.0)
+    turn = np.array([1, 1j, -1, -1j])[order % 4]
+    into = 2 * np.sqrt(order + 0.5) * turn * j * np.exp(-1j * np.pi * offset / (2 * WIDTH))[:, None]
+    into = np.block([[into.real, into.imag], [-into.imag, into.real]])
+    lag = np.arange(LAGS) - LAGS // 2
+    t = (lag + 0.5) / reach
+    legendre = np.ones((TERMS, LAGS))
+    legendre[1] = t
+    for n in range(1, TERMS - 1):
+        legendre[n + 1] = ((2 * n + 1) * t * legendre[n] - n * legendre[n - 1]) / (n + 1)
+    legendre *= np.sqrt(order + 0.5)[:, None]
+    centre = 2 * QUARTER * np.arange(NX) + QUARTER - 1
+    angle = (centre[:, None] * lag[None, :]) % (4 * WIDTH) * (2 * np.pi / (4 * WIDTH))
+    carrier = np.stack([np.cos(angle), np.sin(angle)]) / np.sqrt(WIDTH)
+    return into, legendre, carrier
 
 
 def kernel(
-    spectra_hbm, table_hbm, pairs_hbm, counts, fine_hbm, coarse_hbm, out,
-    spectra, pairs, terms, sums, white32, quarters, held, work, stage, landed, wide, stack, lhs, wave, total, half_out, half_in, parts_out, parts_in,
-    table_all, table_smem, fine, coarse,
+    spectra_hbm, table_hbm, pairs_hbm, counts, into_hbm, legendre_hbm, carrier_hbm, out,
+    spectra, pairs, terms, sums, white32, quarters, held, work, stage, landed, wide, stack, lhs, total, parts_out, parts_in,
+    table_all, table_smem, into, legendre, carrier,
     far, stage_far, table_far, table_far_smem, f_send, f_recv,
-    x_send, x_recv, z_send, z_recv, t_send, t_recv, y_send, y_recv, h_send, h_recv, r_send, r_recv, local_sem, smem_sem,
+    x_send, x_recv, z_send, z_recv, t_send, t_recv, y_send, y_recv, r_send, r_recv, local_sem, smem_sem,
 ):
     win = lax.axis_index("win")
     sta = lax.axis_index("sta")
@@ -102,11 +124,13 @@
     load_table.start()
     load_pairs = pltpu.make_async_copy(pairs_hbm, pairs, local_sem.at[4])
     load_pairs.start()
-    load_fine = pltpu.make_async_copy(fine_hbm, fine, local_sem.at[0])
-    load_fine.start()
-    own_coarse = coarse_hbm.at[:, pl.ds(pl.multiple_of(win * FINE, FINE), FINE)]
-    load_coarse = pltpu.make_async_copy(own_coarse, coarse, local_sem.at[1])
-    load_coarse.start()
+    loads = [
+        pltpu.make_async_copy(into_hbm, into, local_sem.at[0]),
+        pltpu.make_async_copy(legendre_hbm, legendre, local_sem.at[1]),
+        pltpu.make_async_copy(carrier_hbm, carrier, local_sem.at[5]),
+    ]
+    for load in loads:
+        load.start()
 
     lane_r = lax.rem(lax.broadcasted_iota(jnp.int32, (3 * 128, 128), 0), 128) // BAND
     lane_c = lax.broadcasted_iota(jnp.int32, (3 * 128, 128), 1) // BAND
@@ -259,18 +283,6 @@
 
         for c in range(CAP):
             landed[i, place * CAP + c] = stage_far[at, 0, c]
-
-    def make_wave(step):
-        count = QUARTER // FINE // WAVE_STEPS
-
-        @pl.loop(step * count, (step + 1) * count)
-        def _(j):
-            cc = coarse[0, pl.ds(j, 1), :]
-            sc = coarse[1, pl.ds(j, 1), :]
-            rows = pl.ds(pl.multiple_of(j * FINE, FINE), FINE)
-            later = pl.ds(pl.multiple_of(QUARTER + j * FINE, FINE), FINE)
-            wave[rows, :] = (cc * fine[0] - sc * fine[1]).astype(jnp.bfloat16)
-            wave[later, :] = (-(sc * fine[0] + cc * fine[1])).astype(jnp.bfloat16)
 
     half = NZ // 2
     for step in (1, 3, 2):
@@ -350,74 +362,51 @@
             pick_far(i)
         elif kind == "c":
             cross(i)
-        elif kind == "w":
-            if i == 0:
-                load_fine.wait()
-                load_coarse.wait()
-            make_wave(i)
 
     for j in range(2 * ROWS):
         lhs[:, j * 128 : (j + 1) * 128] = stack[pl.ds(j, SLOTS, stride=2 * ROWS), :].astype(jnp.bfloat16)
 
-    sides = ((0, 1), (1, NX - 1))
-    part = SHARE // 2
-
-    def h_copy(side, step, n):
-        return pltpu.make_async_remote_copy(
-            src_ref=half_out.at[side, n], dst_ref=half_in.at[side, n],
-            send_sem=h_send.at[side, n], recv_sem=h_recv.at[side, n],
+    def r_copy(step, n):
+        rows = pl.ds(n * SHARE, SHARE)
+        return pltpu.make_async_remote_copy(
+            src_ref=parts_out.at[step - 1, rows], dst_ref=parts_in.at[step, rows],
+            send_sem=r_send.at[step - 1, n], recv_sem=r_recv.at[step - 1, n],
             device_id=at_x(step), device_id_type=MESH,
         )
 
-    def r_copy(side, step, n, late):
-        first = side * part if late else (1 - side) * part
-        return pltpu.make_async_remote_copy(
-            src_ref=parts_out.at[side, n, pl.ds(first, part)], dst_ref=parts_in.at[side, n, pl.ds(first, part)],
-            send_sem=r_send.at[side, n, int(late)], recv_sem=r_recv.at[side, n, int(late)],
-            device_id=at_x(step), device_id_type=MESH,
-        )
-
-    def block(n, step, first, count):
-        base = lax.rem(win + step, NX) * SHARE + first
-        return total[n, pl.ds(pl.multiple_of(base, count), count), :]
-
-    steps = LAGS // LAG_STEP
-    for n in range(steps):
-        columns = slice(n * LAG_STEP, (n + 1) * LAG_STEP)
-        total[n] = jnp.dot(lhs[...], wave[:, columns], preferred_element_type=jnp.float32)
-        for side, step in sides:
-            half_out[side, n] = block(n, 2, side * part, part).astype(jnp.bfloat16)
-            h_copy(side, step, n).start()
-    for n in range(steps):
-        for side, step in sides:
-            first = (1 - side) * part
-            parts_out[side, n, first : first + part] = block(n, step, first, part).astype(jnp.bfloat16)
-            r_copy(side, step, n, False).start()
-    for n in range(steps):
-        for side, step in sides:
-            first = side * part
-            h_copy(side, step, n).wait_recv()
-            value = block(n, step, first, part) + half_in[side, n].astype(jnp.float32)
-            parts_out[side, n, first : first + part] = value.astype(jnp.bfloat16)
-            r_copy(side, step, n, True).start()
-
-    live = win * SHARE + lax.broadcasted_iota(jnp.int32, (SHARE, LAG_STEP), 0) < counts[0]
-    for n in range(steps):
-        value = block(n, 0, 0, SHARE)
-        for side, step in sides:
-            for late in (False, True):
-                r_copy(side, step, n, late).wait_recv()
-            value = value + parts_in[side, n].astype(jnp.float32)
-        value = value * (1.0 / math.sqrt(WIDTH))
-        out[:, n * LAG_STEP : (n + 1) * LAG_STEP] = jnp.where(live, value, 0.0)
+    for load in loads:
+        load.wait()
+    for n in range(2):
+        total[...] = jnp.dot(
+            lhs[...], into[:, n * TERMS : (n + 1) * TERMS], preferred_element_type=jnp.float32
+        )
+        for step in (2, 1, 3, 0):
+            rows = pl.ds(pl.multiple_of(lax.rem(win + step, NX) * SHARE, SHARE), SHARE)
+            part = total[rows, :].astype(jnp.bfloat16)
+            if step == 0:
+                parts_in[0, n * SHARE : (n + 1) * SHARE] = part
+            else:
+                parts_out[step - 1, n * SHARE : (n + 1) * SHARE] = part
+                r_copy(step, n).start()
+
+    live = win * SHARE + lax.broadcasted_iota(jnp.int32, (SHARE, LAGS), 0) < counts[0]
+    value = jnp.zeros((SHARE, LAGS), jnp.float32)
+    for step in (0, 1, 3, 2):
+        if step > 0:
+            for n in range(2):
+                r_copy(step, n).wait_recv()
+        waves = jnp.dot(parts_in[step], legendre[0], preferred_element_type=jnp.float32)
+        waves += jnp.dot(parts_in[step], legendre[1], preferred_element_type=jnp.float32)
+        quarter = lax.rem(win - step + NX, NX)
+        cos = carrier[0, pl.ds(quarter, 1), :]
+        sin = carrier[1, pl.ds(quarter, 1), :]
+        value = value + (waves[:SHARE] * cos - waves[SHARE:] * sin)
+    out[...] = jnp.where(live, value, 0.0)
 
     for step in (1, 2, 3):
         x_copy(step).wait_send()
-    for side, step in sides:
-        for n in range(steps):
-            h_copy(side, step, n).wait_send()
-            for late in (False, True):
-                r_copy(side, step, n, late).wait_send()
+        for n in range(2):
+            r_copy(step, n).wait_send()
     for i in range(NX):
         arrived = landed.at[i, pl.ds(0, sent(i))]
         pltpu.make_async_copy(arrived, arrived, y_send.at[i]).wait()
@@ -436,21 +425,23 @@
 
 def local(spectra, wanted, pairs, counts):
     table = jnp.transpose(wanted, (2, 0, 1))
-    fine, coarse = tables()
+    into, legendre, carrier = expansion()
+    high = legendre.astype(jnp.bfloat16)
+    low = (legendre - high.astype(np.float64)).astype(jnp.bfloat16)
+    constants = [into.astype(jnp.bfloat16), np.stack([high, low]), carrier.astype(np.float32)]
     vmem = pl.BlockSpec(memory_space=pltpu.VMEM)
     smem = pl.BlockSpec(memory_space=pltpu.SMEM)
     hbm = pl.BlockSpec(memory_space=pltpu.HBM)
     half = NZ // 2
-    steps = LAGS // LAG_STEP
     bf16, f32 = jnp.bfloat16, jnp.float32
     dma = pltpu.SemaphoreType.DMA
     held_in_hbm = [
-        pltpu.with_memory_space_constraint(jnp.asarray(x), pltpu.HBM) for x in (spectra[0], table, pairs.T, fine, coarse)
+        pltpu.with_memory_space_constraint(jnp.asarray(x), pltpu.HBM) for x in (spectra[0], table, pairs.T, *constants)
     ]
     return pl.pallas_call(
         kernel,
         out_shape=jax.ShapeDtypeStruct((SHARE, LAGS), f32),
-        in_specs=[hbm, hbm, hbm, smem, hbm, hbm],
+        in_specs=[hbm, hbm, hbm, smem, hbm, hbm, hbm],
         out_specs=vmem,
         scratch_shapes=[
             pltpu.VMEM((STATIONS, 2 * WIDTH), f32),
@@ -466,16 +457,14 @@
             pltpu.VMEM((RECV, 2 * ROWS, 128), f32),
             pltpu.VMEM((SLOTS * 2 * ROWS, 128), f32),
             pltpu.VMEM((SLOTS, 2 * QUARTER), bf16),
-            pltpu.VMEM((2 * QUARTER, LAGS), bf16),
-            pltpu.VMEM((steps, SLOTS, LAG_STEP), f32),
-            pltpu.VMEM((2, steps, SHARE // 2, LAG_STEP), bf16),
-            pltpu.VMEM((2, steps, SHARE // 2, LAG_STEP), bf16),
-            pltpu.VMEM((2, steps, SHARE, LAG_STEP), bf16),
-            pltpu.VMEM((2, steps, SHARE, LAG_STEP), bf16),
+            pltpu.VMEM((SLOTS, TERMS), f32),
+            pltpu.VMEM((NX - 1, 2 * SHARE, TERMS), bf16),
+            pltpu.VMEM((NX, 2 * SHARE, TERMS), bf16),
             pltpu.VMEM((NZ, CAP, 1, NZ * YC), jnp.int32),
             pltpu.SMEM((NZ, CAP, 1, NZ * YC), jnp.int32),
-            pltpu.VMEM((2, FINE, LAGS), f32),
-            pltpu.VMEM((2, QUARTER // FINE, LAGS), f32),
+            pltpu.VMEM((2 * QUARTER, 2 * TERMS), bf16),
+            pltpu.VMEM((2, TERMS, LAGS), bf16),
+            pltpu.VMEM((2, NX, LAGS), f32),
             pltpu.VMEM((max(len(FAR), 1), STATIONS, 2 * ROWS, 128), bf16),
             pltpu.VMEM((max(len(FAR), 1), NEAR * NC, CAP, 2 * ROWS, 128), bf16),
             pltpu.VMEM((CAP, 1, NZ * YC), jnp.int32),
@@ -485,9 +474,8 @@
             dma((NX, 2, half)), dma((NX, 2, half)),
             dma((2, half)), dma((2, half)),
             dma((NX,)), dma((NX,)),
-            dma((2, steps)), dma((2, steps)),
-            dma((2, steps, 2)), dma((2, steps, 2)),
-            dma((5,)), dma((NZ + 1,)),
+            dma((NX - 1, 2)), dma((NX - 1, 2)),
+            dma((6,)), dma((NZ + 1,)),
         ],
         compiler_params=pltpu.CompilerParams(
             collective_id=0, has_side_effects=True, vmem_limit_bytes=48 << 20

time: 57.3 us -> 55.9 us (0.976)
  Pallas kernels: 55.9 us -> 54.5 us
    pallas_call x1, Pallas kernels: 55.9 us -> 54.5 us  [local(): pl.pallas_call(kernel, out_shape=jax.ShapeDtypeStruct((SHARE, LAGS), f32)...]
where the time goes in v4:
time: 55.9 us
  Pallas kernels  54.5 us (97%)
  local copies, waits for them, and re-layouts  0.71 us (1%)
  between operations  0.66 us (1%)
    pallas_call x1, Pallas kernels, local(): pl.pallas_call(kernel, out_shape=jax.ShapeDtypeStruct((SHARE, LAGS), f32)...  54.5 us

profile of v4, /device:TPU:1, one launch (start us, length us, event | category | flops | bytes accessed | tf_op | source)
XLA Modules:
  0.0 55.9 jit_solution(11611160749313714679)
XLA Ops:
  0.7 54.5 %correlate.1 = f32[64,1024]{1,0:T(8,128)S(1)} custom-call(f32[16,8192]{1,0:T(8,128)} %bitcast.3, s32[3,1,64]{2,1,0:T(1,128)} %bitcast.5, s32[2,256]{1,0:T(2,128)} %bitcast.4, s32[1]{0:T(128)S(6)} %copy.9.counts, bf16[2048,512]{1,0:T(8,128)(2,1)} %constant.6.clone.into_hbm, bf16[2,256,1024]{2,1,0:T(8,128)(2,1)} %constant.7.clone.legendre_hbm, ...), custom_call_target="tpu_custom_call" | custom-call | tf_op jit(solution)/shard_map/correlate/pallas_call | solution.py:441
  55.2 0.7 %copy.10 = f32[64,1024]{1,0:T(8,128)} copy(f32[64,1024]{1,0:T(8,128)S(1)} %correlate.1) | data formatting | bytes 524288

commit v5 on v4

--- a/solution.py
+++ b/solution.py
@@ -22,18 +22,17 @@
 RECV = NZ * YC * CAP
 TERMS = 256
 SHIFT = (0, 1, 3, 2)
-FAR = (0, 1)
-REACH = 3
-NEAR = 1 + 2 * REACH
+REACH = {0: 2, 1: 3, 2: 3}
+FAR = tuple(REACH)
 ORDER = (
-    "x0", "p00", "z01", "p01", "x1", "p10", "x2", "p20", "z02", "x3", "p30",
-    "p02", "z11", "p11", "z21", "p21", "z31", "p31", "z03", "z12", "p03", "z22",
-    "p22", "p12", "z04", "z32", "p04", "z13", "z23", "p13", "p23", "z33", "z14",
-    "f0", "z24", "z34", "p14", "p24", "p33", "p32", "f1", "p34", "c0", "c2",
-    "c1", "c3",
+    "x0", "p00", "z01", "x2", "p01", "x1", "x3", "p30", "z02", "p10", "p02", "p20",
+    "z21", "p21", "z31", "p31", "z03", "z22", "p22", "z11", "p11", "z32", "p32", "z23",
+    "z04", "p04", "z12", "p03", "f0", "z33", "p33", "z13", "z24", "f2", "p24", "p23",
+    "z14", "z34", "p34", "p14", "f1", "p13", "c0", "p12", "c2", "c3", "c1",
 )
 FIRST_FAR = [int(event[1]) for event in ORDER if event[0] == "f"][:1]
-FIRST_CROSS = [int(event[1]) for event in ORDER if event[0] == "c"][:1]
+CROSSES = [int(event[1]) for event in ORDER if event[0] == "c"]
+SENDS = (2, 1, 3, 0)
 MESH = pl.DeviceIdType.MESH
 
 
@@ -75,11 +74,13 @@
 
 def kernel(
     spectra_hbm, table_hbm, pairs_hbm, counts, into_hbm, legendre_hbm, carrier_hbm, out,
-    spectra, pairs, terms, sums, white32, quarters, held, work, stage, landed, wide, stack, lhs, total, parts_out, parts_in,
+    spectra, pairs, pairs_raw, pairs_here, terms, sums, white32, quarters, held, work, stage, landed_0, landed_1, landed_2, landed_3, stack_0, stack_1, lhs, total, parts_out, parts_in,
     table_all, table_smem, into, legendre, carrier,
     far, stage_far, table_far, table_far_smem, f_send, f_recv,
     x_send, x_recv, z_send, z_recv, t_send, t_recv, y_send, y_recv, r_send, r_recv, local_sem, smem_sem,
 ):
+    landed = (landed_0, landed_1, landed_2, landed_3)
+    stacks = (stack_0, stack_1)
     win = lax.axis_index("win")
     sta = lax.axis_index("sta")
     z = sta // YC
@@ -99,8 +100,8 @@
         return to, (z * YC + to, win)
 
     def at_zc(step):
-        along = step // NC
-        along = along + jnp.where(along > REACH, NZ - NEAR, 0)
+        place = step // NC
+        along = jnp.where(lax.rem(place, 2) == 1, (place + 1) // 2, NZ - place // 2)
         to = lax.rem(z + along, NZ) * YC + y * NC + lax.rem(core + lax.rem(step, NC), NC)
         return to, (to, win)
 
@@ -115,14 +116,16 @@
         pl.semaphore_signal(barrier, inc=1, device_id=at_x(step), device_id_type=MESH)
     for step in range(1, YC):
         pl.semaphore_signal(barrier, inc=1, device_id=at_yc(step)[1], device_id_type=MESH)
-    for step in range(NC, NEAR * NC):
+    farthest = 1 + 2 * max(REACH.values())
+    for step in range(NC, farthest * NC):
         pl.semaphore_signal(barrier, inc=1, device_id=at_zc(step)[1], device_id_type=MESH)
 
     load_spectra = pltpu.make_async_copy(spectra_hbm, spectra, local_sem.at[2])
     load_spectra.start()
     load_table = pltpu.make_async_copy(table_hbm, table_all.at[z], local_sem.at[3])
     load_table.start()
-    load_pairs = pltpu.make_async_copy(pairs_hbm, pairs, local_sem.at[4])
+    load_pairs = pltpu.make_async_copy(pairs_hbm, pairs_raw, local_sem.at[4])
+    pairs_to_smem = pltpu.make_async_copy(pairs_here, pairs, local_sem.at[6])
     load_pairs.start()
     loads = [
         pltpu.make_async_copy(into_hbm, into, local_sem.at[0]),
@@ -170,8 +173,7 @@
 
     load_table.wait()
     to_smem(z).start()
-    load_pairs.wait()
-    pl.semaphore_wait(barrier, 3 + YC - 1 + NEAR * NC - NC)
+    pl.semaphore_wait(barrier, 3 + YC - 1 + farthest * NC - NC)
 
     def x_copy(step):
         place = SHIFT.index((NX - step) % NX)
@@ -228,12 +230,21 @@
             device_id=(z * YC + across, win), device_id_type=MESH,
         )
 
-    def pick(i, source, k):
-        for s in range(STATIONS):
-            work[s] = held[i, source, s]
-        place = source * YC + yc
-
-        skip = i in FAR and k <= REACH
+    half = NZ // 2
+
+    def pick(i, k):
+        sources = [lax.rem(z - k + NZ, NZ)]
+        if 0 < k < half:
+            sources.append(lax.rem(z + k, NZ))
+        if i == 0:
+            for source in sources:
+                to_smem(source).wait()
+        for n, source in enumerate(sources):
+            for s in range(STATIONS):
+                work[n, s] = held[i, source, s]
+        count = CAP * len(sources)
+        place = (yc * NZ + max(2 * k - 1, 0)) * CAP
+        skip = i in FAR and k <= REACH[i]
 
         @pl.loop(0, YC - NC if skip else YC)
         def _(turn):
@@ -241,20 +252,21 @@
             if skip:
                 step = turn + jnp.where(turn >= YC // 2, NC, 0)
             to, device = at_yc(step)
-            for c in range(CAP):
-                wanted = table_smem[source, c, 0, z * YC + to]
-                stage[i, source, step, c] = work[wanted]
+            for n, source in enumerate(sources):
+                for c in range(CAP):
+                    wanted = table_smem[source, c, 0, z * YC + to]
+                    stage[i, k, step, n * CAP + c] = work[n, wanted]
 
             @pl.when(step > 0)
             def _():
                 pltpu.make_async_remote_copy(
-                    src_ref=stage.at[i, source, step], dst_ref=landed.at[i, pl.ds(place * CAP, CAP)],
+                    src_ref=stage.at[i, k, step, pl.ds(0, count)], dst_ref=landed[i].at[pl.ds(place, count)],
                     send_sem=y_send.at[i], recv_sem=y_recv.at[i],
                     device_id=device, device_id_type=MESH,
                 ).start()
 
-        for c in range(CAP):
-            landed[i, place * CAP + c] = stage[i, source, 0, c]
+        for c in range(count):
+            landed[i][place + c] = stage[i, k, 0, c]
 
     def pick_far(i):
         at = FAR.index(i)
@@ -264,27 +276,35 @@
             far_to_smem().wait()
         far_copy(i).wait_recv()
         for s in range(STATIONS):
-            work[s] = far[at, s]
-        place = z * YC + across
-
-        @pl.loop(0, NEAR * NC)
+            work[0, s] = far[at, s]
+        place = across * NZ * CAP
+
+        @pl.loop(0, (1 + 2 * REACH[i]) * NC)
         def _(step):
             to, device = at_zc(step)
             for c in range(CAP):
-                stage_far[at, step, c] = work[table_far_smem[c, 0, to]]
+                stage_far[at, step, c] = work[0, table_far_smem[c, 0, to]]
 
             @pl.when(step > 0)
             def _():
                 pltpu.make_async_remote_copy(
-                    src_ref=stage_far.at[at, step], dst_ref=landed.at[i, pl.ds(place * CAP, CAP)],
+                    src_ref=stage_far.at[at, step], dst_ref=landed[i].at[pl.ds(place + step // NC * CAP, CAP)],
                     send_sem=y_send.at[i], recv_sem=y_recv.at[i],
                     device_id=device, device_id_type=MESH,
                 ).start()
 
         for c in range(CAP):
-            landed[i, place * CAP + c] = stage_far[at, 0, c]
-
-    half = NZ // 2
+            landed[i][place + c] = stage_far[at, 0, c]
+
+    def move_pairs():
+        load_pairs.wait()
+        entry = pairs_raw[...]
+        source = entry // CAP
+        distance = lax.rem(source // YC - z + NZ, NZ)
+        nearness = jnp.where(distance < half, 2 * distance, 2 * NZ - 1 - 2 * distance)
+        pairs_here[...] = (lax.rem(source, YC) * NZ + nearness) * CAP + lax.rem(entry, CAP)
+        pairs_to_smem.start()
+
     for step in (1, 3, 2):
         x_copy(step).start()
     for way in (1, -1):
@@ -296,36 +316,38 @@
         far_table_copy().start()
 
     def sent(i):
-        direct = NZ * (YC - 1)
-        return CAP * (direct - NEAR * NC + NEAR * NC - 1 if i in FAR else direct)
+        return CAP * (NZ * (YC - 1) - (1 if i in FAR else 0))
 
     def cross(i):
-        arrived = landed.at[i, pl.ds(0, sent(i))]
+        if i == CROSSES[0]:
+            pairs_to_smem.wait()
+        arrived = landed[i].at[pl.ds(0, sent(i))]
         pltpu.make_async_copy(arrived, arrived, y_recv.at[i]).wait()
 
-        @pl.loop(0, RECV // 8)
-        def _(g):
-            for e in range(8):
-                wide[g * 8 + e] = landed[i, g * 8 + e].astype(jnp.float32)
-
-        @pl.loop(0, SLOTS // 8)
-        def _(g):
-            for e in range(8):
-                p = g * 8 + e
-                left = wide[pairs[0, p]]
-                right = wide[pairs[1, p]]
-                lre, lim = left[:ROWS], left[ROWS:]
-                rre, rim = right[:ROWS], right[ROWS:]
-                re = lre * rre + lim * rim
-                im = lre * rim - lim * rre
-                first = pl.ds(pl.multiple_of(p * 2 * ROWS, ROWS), ROWS)
-                second = pl.ds(pl.multiple_of(p * 2 * ROWS + ROWS, ROWS), ROWS)
-                if [i] == FIRST_CROSS:
-                    stack[first, :] = re
-                    stack[second, :] = im
-                else:
-                    stack[first, :] += re
-                    stack[second, :] += im
+        source = landed[i]
+        turn = CROSSES.index(i)
+        before, after = stacks[(turn + 1) % 2], stacks[turn % 2]
+        for b, step in enumerate(SENDS):
+            base = lax.rem(win + step, NX) * SHARE
+
+            @pl.loop(0, SHARE // 16)
+            def _(g):
+                for e in range(16):
+                    p = base + g * 16 + e
+                    left = source[pairs[0, p]].astype(jnp.float32)
+                    right = source[pairs[1, p]].astype(jnp.float32)
+                    lre, lim = left[:ROWS], left[ROWS:]
+                    rre, rim = right[:ROWS], right[ROWS:]
+                    re = lre * rre + lim * rim
+                    im = lre * rim - lim * rre
+                    row = (b * SHARE + g * 16 + e) * 2 * ROWS
+                    first = pl.ds(pl.multiple_of(row, ROWS), ROWS)
+                    second = pl.ds(pl.multiple_of(row + ROWS, ROWS), ROWS)
+                    if turn > 0:
+                        re += before[first, :]
+                        im += before[second, :]
+                    after[first, :] = re
+                    after[second, :] = im
 
     for event in ORDER:
         kind, i = event[0], int(event[1])
@@ -351,50 +373,50 @@
                     if k < half - 1:
                         t_copy(-1, k).start()
         elif kind == "p":
-            sources = [lax.rem(z - k + NZ, NZ)]
-            if 0 < k < half:
-                sources.append(lax.rem(z + k, NZ))
-            for source in sources:
-                if i == 0:
-                    to_smem(source).wait()
-                pick(i, source, k)
+            pick(i, k)
+            if (i, k) == (0, 1):
+                move_pairs()
         elif kind == "f":
             pick_far(i)
         elif kind == "c":
             cross(i)
 
-    for j in range(2 * ROWS):
-        lhs[:, j * 128 : (j + 1) * 128] = stack[pl.ds(j, SLOTS, stride=2 * ROWS), :].astype(jnp.bfloat16)
-
-    def r_copy(step, n):
-        rows = pl.ds(n * SHARE, SHARE)
+    def r_copy(step):
         return pltpu.make_async_remote_copy(
-            src_ref=parts_out.at[step - 1, rows], dst_ref=parts_in.at[step, rows],
-            send_sem=r_send.at[step - 1, n], recv_sem=r_recv.at[step - 1, n],
+            src_ref=parts_out.at[step - 1], dst_ref=parts_in.at[step],
+            send_sem=r_send.at[step - 1], recv_sem=r_recv.at[step - 1],
             device_id=at_x(step), device_id_type=MESH,
         )
 
     for load in loads:
         load.wait()
-    for n in range(2):
-        total[...] = jnp.dot(
-            lhs[...], into[:, n * TERMS : (n + 1) * TERMS], preferred_element_type=jnp.float32
-        )
-        for step in (2, 1, 3, 0):
-            rows = pl.ds(pl.multiple_of(lax.rem(win + step, NX) * SHARE, SHARE), SHARE)
-            part = total[rows, :].astype(jnp.bfloat16)
-            if step == 0:
-                parts_in[0, n * SHARE : (n + 1) * SHARE] = part
-            else:
-                parts_out[step - 1, n * SHARE : (n + 1) * SHARE] = part
-                r_copy(step, n).start()
+    stack = stacks[(NX - 1) % 2]
+    for side in range(2):
+        rows = slice(side * 2 * SHARE, (side + 1) * 2 * SHARE)
+        for j in range(2 * ROWS):
+            strided = pl.ds(side * 2 * SHARE * 2 * ROWS + j, 2 * SHARE, stride=2 * ROWS)
+            lhs[rows, j * 128 : (j + 1) * 128] = stack[strided, :].astype(jnp.bfloat16)
+        for n in range(2):
+            total[...] = jnp.dot(
+                lhs[rows, :], into[:, n * TERMS : (n + 1) * TERMS], preferred_element_type=jnp.float32
+            )
+            for b in range(2):
+                step = SENDS[2 * side + b]
+                part = total[b * SHARE : (b + 1) * SHARE, :].astype(jnp.bfloat16)
+                place = slice(n * SHARE, (n + 1) * SHARE)
+                if step == 0:
+                    parts_in[0, place] = part
+                else:
+                    parts_out[step - 1, place] = part
+        for b in range(2):
+            if SENDS[2 * side + b]:
+                r_copy(SENDS[2 * side + b]).start()
 
     live = win * SHARE + lax.broadcasted_iota(jnp.int32, (SHARE, LAGS), 0) < counts[0]
     value = jnp.zeros((SHARE, LAGS), jnp.float32)
     for step in (0, 1, 3, 2):
         if step > 0:
-            for n in range(2):
-                r_copy(step, n).wait_recv()
+            r_copy(step).wait_recv()
         waves = jnp.dot(parts_in[step], legendre[0], preferred_element_type=jnp.float32)
         waves += jnp.dot(parts_in[step], legendre[1], preferred_element_type=jnp.float32)
         quarter = lax.rem(win - step + NX, NX)
@@ -405,10 +427,9 @@
 
     for step in (1, 2, 3):
         x_copy(step).wait_send()
-        for n in range(2):
-            r_copy(step, n).wait_send()
+        r_copy(step).wait_send()
     for i in range(NX):
-        arrived = landed.at[i, pl.ds(0, sent(i))]
+        arrived = landed[i].at[pl.ds(0, sent(i))]
         pltpu.make_async_copy(arrived, arrived, y_send.at[i]).wait()
         for way in (1, -1):
             for k in range(half):
@@ -430,8 +451,8 @@
     low = (legendre - high.astype(np.float64)).astype(jnp.bfloat16)
     constants = [into.astype(jnp.bfloat16), np.stack([high, low]), carrier.astype(np.float32)]
     vmem = pl.BlockSpec(memory_space=pltpu.VMEM)
+    hbm = pl.BlockSpec(memory_space=pltpu.HBM)
     smem = pl.BlockSpec(memory_space=pltpu.SMEM)
-    hbm = pl.BlockSpec(memory_space=pltpu.HBM)
     half = NZ // 2
     bf16, f32 = jnp.bfloat16, jnp.float32
     dma = pltpu.SemaphoreType.DMA
@@ -441,23 +462,24 @@
     return pl.pallas_call(
         kernel,
         out_shape=jax.ShapeDtypeStruct((SHARE, LAGS), f32),
-        in_specs=[hbm, hbm, hbm, smem, hbm, hbm, hbm],
+        in_specs=[hbm] * 3 + [smem] + [hbm] * 3,
         out_specs=vmem,
         scratch_shapes=[
             pltpu.VMEM((STATIONS, 2 * WIDTH), f32),
             pltpu.SMEM((2, SLOTS), jnp.int32),
+            pltpu.VMEM((2, SLOTS), jnp.int32),
+            pltpu.VMEM((2, SLOTS), jnp.int32),
             pltpu.VMEM((STATIONS * WIDTH // 128, 3 * 128), bf16),
             pltpu.VMEM((STATIONS * WIDTH // 128, 128), f32),
             pltpu.VMEM((STATIONS * 2 * (WIDTH // 128), 128), f32),
             pltpu.VMEM((NX - 1, STATIONS, 2 * ROWS, 128), bf16),
             pltpu.VMEM((NX, NZ, STATIONS, 2 * ROWS, 128), bf16),
-            pltpu.VMEM((STATIONS, 2 * ROWS, 128), bf16),
-            pltpu.VMEM((NX, NZ, YC, CAP, 2 * ROWS, 128), bf16),
-            pltpu.VMEM((NX, RECV, 2 * ROWS, 128), bf16),
-            pltpu.VMEM((RECV, 2 * ROWS, 128), f32),
-            pltpu.VMEM((SLOTS * 2 * ROWS, 128), f32),
+            pltpu.VMEM((2, STATIONS, 2 * ROWS, 128), bf16),
+            pltpu.VMEM((NX, half + 1, YC, 2 * CAP, 2 * ROWS, 128), bf16),
+            *[pltpu.VMEM((RECV, 2 * ROWS, 128), bf16)] * NX,
+            *[pltpu.VMEM((SLOTS * 2 * ROWS, 128), f32)] * 2,
             pltpu.VMEM((SLOTS, 2 * QUARTER), bf16),
-            pltpu.VMEM((SLOTS, TERMS), f32),
+            pltpu.VMEM((2 * SHARE, TERMS), f32),
             pltpu.VMEM((NX - 1, 2 * SHARE, TERMS), bf16),
             pltpu.VMEM((NX, 2 * SHARE, TERMS), bf16),
             pltpu.VMEM((NZ, CAP, 1, NZ * YC), jnp.int32),
@@ -465,8 +487,8 @@
             pltpu.VMEM((2 * QUARTER, 2 * TERMS), bf16),
             pltpu.VMEM((2, TERMS, LAGS), bf16),
             pltpu.VMEM((2, NX, LAGS), f32),
-            pltpu.VMEM((max(len(FAR), 1), STATIONS, 2 * ROWS, 128), bf16),
-            pltpu.VMEM((max(len(FAR), 1), NEAR * NC, CAP, 2 * ROWS, 128), bf16),
+            pltpu.VMEM((len(FAR), STATIONS, 2 * ROWS, 128), bf16),
+            pltpu.VMEM((len(FAR), (1 + 2 * max(REACH.values())) * NC, CAP, 2 * ROWS, 128), bf16),
             pltpu.VMEM((CAP, 1, NZ * YC), jnp.int32),
             pltpu.SMEM((CAP, 1, NZ * YC), jnp.int32),
             dma((len(FAR) + 1,)), dma((len(FAR) + 1,)),
@@ -474,8 +496,8 @@
             dma((NX, 2, half)), dma((NX, 2, half)),
             dma((2, half)), dma((2, half)),
             dma((NX,)), dma((NX,)),
-            dma((NX - 1, 2)), dma((NX - 1, 2)),
-            dma((6,)), dma((NZ + 1,)),
+            dma((NX - 1,)), dma((NX - 1,)),
+            dma((7,)), dma((NZ + 1,)),
         ],
         compiler_params=pltpu.CompilerParams(
             collective_id=0, has_side_effects=True, vmem_limit_bytes=48 << 20

time: 55.9 us -> 54.2 us (0.970)
  Pallas kernels: 54.5 us -> 52.7 us
    pallas_call x1, Pallas kernels: 54.5 us -> 52.7 us  [local(): pl.pallas_call(kernel, out_shape=jax.ShapeDtypeStruct((SHARE, LAGS), f32)...]
where the time goes in v5:
time: 54.2 us; the launch traced here: 54.1 us
  Pallas kernels  52.7 us (97%)
  local copies, waits for them, and re-layouts  0.71 us (1%)
  between operations  0.66 us (1%)
    pallas_call x1, Pallas kernels, local(): pl.pallas_call(kernel, out_shape=jax.ShapeDtypeStruct((SHARE, LAGS), f32)...  52.7 us

profile of v5, /device:TPU:1, one launch (start us, length us, event | category | flops | bytes accessed | tf_op | source)
XLA Modules:
  0.0 54.1 jit_solution(18073902200924908106)
XLA Ops:
  0.7 52.7 %correlate.1 = f32[64,1024]{1,0:T(8,128)S(1)} custom-call(f32[16,8192]{1,0:T(8,128)} %bitcast.3, s32[3,1,64]{2,1,0:T(1,128)} %bitcast.5, s32[2,256]{1,0:T(2,128)} %bitcast.4, s32[1]{0:T(128)S(6)} %copy.9.counts, bf16[2048,512]{1,0:T(8,128)(2,1)} %constant.6.clone.into_hbm, bf16[2,256,1024]{2,1,0:T(8,128)(2,1)} %constant.7.clone.legendre_hbm, ...), custom_call_target="tpu_custom_call" | custom-call | tf_op jit(solution)/shard_map/correlate/pallas_call | solution.py:462
  53.4 0.7 %copy.10 = f32[64,1024]{1,0:T(8,128)} copy(f32[64,1024]{1,0:T(8,128)S(1)} %correlate.1) | data formatting | bytes 524288

commit v6 on v5

--- a/solution.py
+++ b/solution.py
@@ -21,14 +21,15 @@
 SHARE = SLOTS // NX
 RECV = NZ * YC * CAP
 TERMS = 256
+PIECES = 4
 SHIFT = (0, 1, 3, 2)
 REACH = {0: 2, 1: 3, 2: 3}
 FAR = tuple(REACH)
 ORDER = (
     "x0", "p00", "z01", "x2", "p01", "x1", "x3", "p30", "z02", "p10", "p02", "p20",
     "z21", "p21", "z31", "p31", "z03", "z22", "p22", "z11", "p11", "z32", "p32", "z23",
-    "z04", "p04", "z12", "p03", "f0", "z33", "p33", "z13", "z24", "f2", "p24", "p23",
-    "z14", "z34", "p34", "p14", "f1", "p13", "c0", "p12", "c2", "c3", "c1",
+    "z04", "p04", "z12", "p12", "p03", "f0", "z33", "p33", "z13", "z24", "f2", "p13",
+    "p24", "p23", "z14", "z34", "p34", "p14", "f1", "c0", "c2", "c3", "c1",
 )
 FIRST_FAR = [int(event[1]) for event in ORDER if event[0] == "f"][:1]
 CROSSES = [int(event[1]) for event in ORDER if event[0] == "c"]
@@ -77,7 +78,7 @@
     spectra, pairs, pairs_raw, pairs_here, terms, sums, white32, quarters, held, work, stage, landed_0, landed_1, landed_2, landed_3, stack_0, stack_1, lhs, total, parts_out, parts_in,
     table_all, table_smem, into, legendre, carrier,
     far, stage_far, table_far, table_far_smem, f_send, f_recv,
-    x_send, x_recv, z_send, z_recv, t_send, t_recv, y_send, y_recv, r_send, r_recv, local_sem, smem_sem,
+    x_send, x_recv, z_send, z_recv, t_send, t_recv, y_send, y_recv, r_send, r_recv, local_sem, spectra_sem, smem_sem,
 ):
     landed = (landed_0, landed_1, landed_2, landed_3)
     stacks = (stack_0, stack_1)
@@ -105,6 +106,18 @@
         to = lax.rem(z + along, NZ) * YC + y * NC + lax.rem(core + lax.rem(step, NC), NC)
         return to, (to, win)
 
+    piece = WIDTH // PIECES
+
+    def load_spectra(n, part):
+        columns = pl.ds(part * WIDTH + n * piece, piece)
+        return pltpu.make_async_copy(
+            spectra_hbm.at[:, columns], spectra.at[:, columns], spectra_sem.at[n, part]
+        )
+
+    for n in range(PIECES):
+        for part in range(2):
+            load_spectra(n, part).start()
+
     def to_smem(source):
         return pltpu.make_async_copy(table_all.at[source], table_smem.at[source], smem_sem.at[source])
 
@@ -120,8 +133,6 @@
     for step in range(NC, farthest * NC):
         pl.semaphore_signal(barrier, inc=1, device_id=at_zc(step)[1], device_id_type=MESH)
 
-    load_spectra = pltpu.make_async_copy(spectra_hbm, spectra, local_sem.at[2])
-    load_spectra.start()
     load_table = pltpu.make_async_copy(table_hbm, table_all.at[z], local_sem.at[3])
     load_table.start()
     load_pairs = pltpu.make_async_copy(pairs_hbm, pairs_raw, local_sem.at[4])
@@ -132,16 +143,16 @@
         pltpu.make_async_copy(legendre_hbm, legendre, local_sem.at[1]),
         pltpu.make_async_copy(carrier_hbm, carrier, local_sem.at[5]),
     ]
-    for load in loads:
-        load.start()
 
     lane_r = lax.rem(lax.broadcasted_iota(jnp.int32, (3 * 128, 128), 0), 128) // BAND
     lane_c = lax.broadcasted_iota(jnp.int32, (3 * 128, 128), 1) // BAND
     same = jnp.where(lane_r == lane_c, 1.0, 0.0).astype(jnp.bfloat16)
     chunks = WIDTH // 128
-    load_spectra.wait()
 
     for j in range(chunks):
+        if j % (chunks // PIECES) == 0:
+            for part in range(2):
+                load_spectra(j // (chunks // PIECES), part).wait()
         re = spectra[:, j * 128 : (j + 1) * 128]
         im = spectra[:, WIDTH + j * 128 : WIDTH + (j + 1) * 128]
         rest = jnp.sqrt(re * re + im * im)
@@ -252,10 +263,13 @@
             if skip:
                 step = turn + jnp.where(turn >= YC // 2, NC, 0)
             to, device = at_yc(step)
-            for n, source in enumerate(sources):
-                for c in range(CAP):
-                    wanted = table_smem[source, c, 0, z * YC + to]
-                    stage[i, k, step, n * CAP + c] = work[n, wanted]
+            picked = [
+                work[n, table_smem[source, c, 0, z * YC + to]]
+                for n, source in enumerate(sources)
+                for c in range(CAP)
+            ]
+            for c in range(count):
+                stage[i, k, step, c] = picked[c]
 
             @pl.when(step > 0)
             def _():
@@ -282,8 +296,9 @@
         @pl.loop(0, (1 + 2 * REACH[i]) * NC)
         def _(step):
             to, device = at_zc(step)
+            picked = [work[0, table_far_smem[c, 0, to]] for c in range(CAP)]
             for c in range(CAP):
-                stage_far[at, step, c] = work[0, table_far_smem[c, 0, to]]
+                stage_far[at, step, c] = picked[c]
 
             @pl.when(step > 0)
             def _():
@@ -305,7 +320,7 @@
         pairs_here[...] = (lax.rem(source, YC) * NZ + nearness) * CAP + lax.rem(entry, CAP)
         pairs_to_smem.start()
 
-    for step in (1, 3, 2):
+    for step in (1, 3):
         x_copy(step).start()
     for way in (1, -1):
         z_copy(0, way, 0).start()
@@ -374,8 +389,12 @@
                         t_copy(-1, k).start()
         elif kind == "p":
             pick(i, k)
+            if (i, k) == (0, 0):
+                x_copy(2).start()
             if (i, k) == (0, 1):
                 move_pairs()
+                for load in loads:
+                    load.start()
         elif kind == "f":
             pick_far(i)
         elif kind == "c":
@@ -412,22 +431,8 @@
             if SENDS[2 * side + b]:
                 r_copy(SENDS[2 * side + b]).start()
 
-    live = win * SHARE + lax.broadcasted_iota(jnp.int32, (SHARE, LAGS), 0) < counts[0]
-    value = jnp.zeros((SHARE, LAGS), jnp.float32)
-    for step in (0, 1, 3, 2):
-        if step > 0:
-            r_copy(step).wait_recv()
-        waves = jnp.dot(parts_in[step], legendre[0], preferred_element_type=jnp.float32)
-        waves += jnp.dot(parts_in[step], legendre[1], preferred_element_type=jnp.float32)
-        quarter = lax.rem(win - step + NX, NX)
-        cos = carrier[0, pl.ds(quarter, 1), :]
-        sin = carrier[1, pl.ds(quarter, 1), :]
-        value = value + (waves[:SHARE] * cos - waves[SHARE:] * sin)
-    out[...] = jnp.where(live, value, 0.0)
-
     for step in (1, 2, 3):
         x_copy(step).wait_send()
-        r_copy(step).wait_send()
     for i in range(NX):
         arrived = landed[i].at[pl.ds(0, sent(i))]
         pltpu.make_async_copy(arrived, arrived, y_send.at[i]).wait()
@@ -442,6 +447,21 @@
         t_copy(1, k).wait_send()
         if k < half - 1:
             t_copy(-1, k).wait_send()
+
+    live = win * SHARE + lax.broadcasted_iota(jnp.int32, (SHARE, LAGS), 0) < counts[0]
+    value = jnp.zeros((SHARE, LAGS), jnp.float32)
+    for step in (0, 1, 3, 2):
+        if step > 0:
+            r_copy(step).wait_recv()
+        waves = jnp.dot(parts_in[step], legendre[0], preferred_element_type=jnp.float32)
+        waves += jnp.dot(parts_in[step], legendre[1], preferred_element_type=jnp.float32)
+        quarter = lax.rem(win - step + NX, NX)
+        cos = carrier[0, pl.ds(quarter, 1), :]
+        sin = carrier[1, pl.ds(quarter, 1), :]
+        value = value + (waves[:SHARE] * cos - waves[SHARE:] * sin)
+    out[...] = jnp.where(live, value, 0.0)
+    for step in (1, 2, 3):
+        r_copy(step).wait_send()
 
 
 def local(spectra, wanted, pairs, counts):
@@ -497,7 +517,7 @@
             dma((2, half)), dma((2, half)),
             dma((NX,)), dma((NX,)),
             dma((NX - 1,)), dma((NX - 1,)),
-            dma((7,)), dma((NZ + 1,)),
+            dma((7,)), dma((PIECES, 2)), dma((NZ + 1,)),
         ],
         compiler_params=pltpu.CompilerParams(
             collective_id=0, has_side_effects=True, vmem_limit_bytes=48 << 20

time: 54.2 us -> 54.2 us (level)
  no operation moved by 1% of the time
where the time goes in v6:
time: 54.2 us; the launch traced here: 54 us
  Pallas kernels  52.7 us (97%)
  local copies, waits for them, and re-layouts  0.71 us (1%)
  between operations  0.66 us (1%)
    pallas_call x1, Pallas kernels, local(): pl.pallas_call(kernel, out_shape=jax.ShapeDtypeStruct((SHARE, LAGS), f32)...  52.7 us

profile of v6, /device:TPU:1, one launch (start us, length us, event | category | flops | bytes accessed | tf_op | source)
XLA Modules:
  0.0 54.0 jit_solution(7836476604127638059)
XLA Ops:
  0.7 52.7 %correlate.1 = f32[64,1024]{1,0:T(8,128)S(1)} custom-call(f32[16,8192]{1,0:T(8,128)} %bitcast.3, s32[3,1,64]{2,1,0:T(1,128)} %bitcast.5, s32[2,256]{1,0:T(2,128)} %bitcast.4, s32[1]{0:T(128)S(6)} %copy.9.counts, bf16[2048,512]{1,0:T(8,128)(2,1)} %constant.6.clone.into_hbm, bf16[2,256,1024]{2,1,0:T(8,128)(2,1)} %constant.7.clone.legendre_hbm, ...), custom_call_target="tpu_custom_call" | custom-call | tf_op jit(solution)/shard_map/correlate/pallas_call | solution.py:482
  53.3 0.7 %copy.10 = f32[64,1024]{1,0:T(8,128)} copy(f32[64,1024]{1,0:T(8,128)S(1)} %correlate.1) | data formatting | bytes 524288

commit v7 on v6

--- a/solution.py
+++ b/solution.py
@@ -259,7 +259,7 @@
 
         @pl.loop(0, YC - NC if skip else YC)
         def _(turn):
-            step = turn
+            step = lax.rem(turn + YC // 2, YC)
             if skip:
                 step = turn + jnp.where(turn >= YC // 2, NC, 0)
             to, device = at_yc(step)
@@ -293,8 +293,11 @@
             work[0, s] = far[at, s]
         place = across * NZ * CAP
 
-        @pl.loop(0, (1 + 2 * REACH[i]) * NC)
-        def _(step):
+        count = (1 + 2 * REACH[i]) * NC
+
+        @pl.loop(0, count)
+        def _(turn):
+            step = count - 1 - turn
             to, device = at_zc(step)
             picked = [work[0, table_far_smem[c, 0, to]] for c in range(CAP)]
             for c in range(CAP):

time: 54.2 us -> 54.4 us (level)
  no operation moved by 1% of the time
where the time goes in v7:
time: 54.4 us; the launch traced here: 54.3 us
  Pallas kernels  52.9 us (97%)
  local copies, waits for them, and re-layouts  0.71 us (1%)
  between operations  0.66 us (1%)
    pallas_call x1, Pallas kernels, local(): pl.pallas_call(kernel, out_shape=jax.ShapeDtypeStruct((SHARE, LAGS), f32)...  52.9 us

profile of v7, /device:TPU:1, one launch (start us, length us, event | category | flops | bytes accessed | tf_op | source)
XLA Modules:
  0.0 54.3 jit_solution(5784797119116576195)
XLA Ops:
  0.7 52.9 %correlate.1 = f32[64,1024]{1,0:T(8,128)S(1)} custom-call(f32[16,8192]{1,0:T(8,128)} %bitcast.3, s32[3,1,64]{2,1,0:T(1,128)} %bitcast.5, s32[2,256]{1,0:T(2,128)} %bitcast.4, s32[1]{0:T(128)S(6)} %copy.9.counts, bf16[2048,512]{1,0:T(8,128)(2,1)} %constant.6.clone.into_hbm, bf16[2,256,1024]{2,1,0:T(8,128)(2,1)} %constant.7.clone.legendre_hbm, ...), custom_call_target="tpu_custom_call" | custom-call | tf_op jit(solution)/shard_map/correlate/pallas_call | solution.py:485
  53.6 0.7 %copy.10 = f32[64,1024]{1,0:T(8,128)} copy(f32[64,1024]{1,0:T(8,128)S(1)} %correlate.1) | data formatting | bytes 524288
